TPU v7x, 128 devices: a whole 4x4x4 slice. The times are simulated.
128 devices in a mesh: dp: 2 (over y_lo), head: 8 (over y_hi, x), space: 8 (over z, core).
Axes of the slice: x: 4, y: 4 (y_hi: 2, y_lo: 2; y = y_hi * 2 + y_lo), z: 4, core: 2. Of those that a mesh axis runs over, the one named last changes fastest.
Arguments:
- features: bfloat16 [2, 64, 64, 1280], P('dp', 'space'), may hold values from -96 to 96
- row_map: int32 [64], replicated, may hold values from 0 to 63, as said below
- head_weights: int32 [2, 8], P('dp', 'head'), may hold values from 1 to 3
- ln_gain: float32 [1280], replicated, may hold values from 0.1 to 1.9
- ln_bias: float32 [1280], replicated, may hold values from -3 to 3
- head_in: bfloat16 [8, 1280, 1024], P('head'), may hold values from -0.15625 to 0.15625
- head_bias: float32 [8, 1024], P('head'), may hold values from -4 to 4
- head_out: float32 [8, 1024], P('head'), may hold values from -0.1875 to 0.1875
- patch_embed: bfloat16 [768, 1280], replicated, may hold values from -0.21875 to 0.21875
- act_in: bfloat16 [2, 1024, 1024, 128], P('dp', 'space', 'head'), may hold values from -6 to 6
- act_mid: bfloat16 [2, 1024, 1024, 128], P('dp', 'space', 'head'), may hold values from -6 to 6
- res_conv: bfloat16 [3, 3, 128, 128], replicated, may hold values from -0.1875 to 0.1875
- out_conv: bfloat16 [3, 3, 128, 3], replicated, may hold values from -1.25 to 1.25
Outputs:
- input_grad: bfloat16 [2, 1024, 1024, 128], P('dp', 'space', 'head')
Inputs may be any that keep to these rules, and one draw needn't show every extreme that they name: `row_map`: a permutation of the patch rows; each 8 consecutive entries hold equally many rows of every block of 8 consecutive patch rows.
All inputs are finite; a program needn't handle non-finite values.
Results may differ from a plain program's by a relative error of at most 0.017.
Values may be sent and summed in bfloat16 or wider, within the bound.
A program may use at most 192 MiB of HBM per device.

v0:
```python
import functools

import jax
import jax.numpy as jnp
import numpy as np
from jax import lax
from jax.experimental import pallas as pl
from jax.experimental.pallas import tpu as pltpu
from jax.sharding import PartitionSpec as P

MESH = pl.DeviceIdType.MESH
PATCH = 16
P3 = 768
HALF = 384
CH = 128
STRIP = 8
PADC = 160
NT = (((1,), (1,)), ((), ()))
SIDES = ((0, 1), (0, -1), (1, 0), (-1, 0), (1, 1), (-1, 1), (1, -1), (-1, -1))


def spread_table():
    table = np.zeros((P3, PATCH * 128), np.float32)
    for o in range(3):
        for a in range(PATCH):
            for b in range(PATCH):
                table[o * 256 + a * 16 + b, b * 128 + 6 + 3 * a + o] = 1
    return table


def tap_table():
    table = np.zeros((PATCH, 256, 32), np.float32)
    for i in range(PATCH):
        for a in range(3):
            for b in range(3):
                for o in range(3):
                    table[i, 64 * b + 3 * (i + a) + o, (a * 3 + b) * 3 + o] = 1
    return table.reshape(PATCH * 256, 32)


def gelu_slope(v):
    bell = jnp.exp(-0.5 * v * v)
    t = 1.0 / (1.0 + 0.2316418882663604 * jnp.abs(v))
    poly = t * (
        0.127414796
        + t * (-0.142248368 + t * (0.7107068705 + t * (-0.7265760135 + t * 0.5307027145)))
    )
    tail = poly * bell
    return jnp.where(v >= 0, 1.0 - tail, tail) + v * bell * 0.3989422804014327


def silu_slope(v):
    t = jnp.tanh(0.5 * v)
    return 0.5 * (1.0 + t) * (1.0 + 0.5 * v * (1.0 - t))


def stack(values):
    return jnp.concatenate([values[:, :HALF], values[:, HALF:]], axis=0)


def unstack(values):
    return jnp.concatenate([values[:8], values[8:]], axis=1)


def trunk_kernel(
    nd,
    nh,
    ns,
    per,
    row_map,
    weight,
    feats,
    gain_ref,
    shift_ref,
    w_hbm,
    hb_ref,
    ho_ref,
    e_hbm,
    act_mid,
    table,
    x_out,
    sdrow_out,
    sdcol_out,
    total_out,
    f_v,
    w_v,
    e_v,
    t_v,
    strip_v,
    strip_f,
    send,
    recv,
    colmsg,
    rowland,
    colland,
    cornerland,
    hmsg,
    hland,
    pm,
    hp,
    sq1,
    sq2,
    load_sem,
    send_sem,
    recv_sem,
    asend_sem,
    arecv_sem,
    hsend_sem,
    hrecv_sem,
    q_sem,
):
    dp, hd, sp = lax.axis_index("dp"), lax.axis_index("head"), lax.axis_index("space")
    rows = ns * PATCH
    group = nh * ns
    me = hd * ns + sp
    barrier = pltpu.get_barrier_semaphore()

    loads = [
        pltpu.make_async_copy(feats.at[0], f_v, load_sem.at[0]),
        pltpu.make_async_copy(w_hbm.at[0], w_v, load_sem.at[1]),
        pltpu.make_async_copy(e_hbm, e_v, load_sem.at[2]),
        pltpu.make_async_copy(act_mid.at[0, :, pl.ds(0, 16)], strip_v.at[0], load_sem.at[3]),
        pltpu.make_async_copy(act_mid.at[0, :, pl.ds(CH - 16, 16)], strip_v.at[1], load_sem.at[4]),
        pltpu.make_async_copy(table, t_v, load_sem.at[5]),
    ]
    for load in loads:
        load.start()

    def greet(i, carry):
        j = lax.rem(me + i, group)
        pl.semaphore_signal(
            barrier, inc=1, device_id=(dp, lax.div(j, ns), lax.rem(j, ns)), device_id_type=MESH
        )
        return carry

    lax.fori_loop(1, group, greet, 0)

    def greet_far(i, carry):
        pl.semaphore_signal(
            barrier,
            inc=1,
            device_id=(lax.rem(dp + 1 + lax.div(i, ns), nd), hd, lax.rem(i, ns)),
            device_id_type=MESH,
        )
        return carry

    lax.fori_loop(0, (nd - 1) * ns, greet_far, 0)

    loads[0].wait()
    gain = gain_ref[...]
    shift = shift_ref[...]
    second = ho_ref[...] * weight[0, 0].astype(jnp.float32)
    first_bias = hb_ref[...]

    def position(k):
        found = jnp.int32(0)
        for p in range(ns):
            found = found + jnp.where(lax.div(row_map[sp * ns + p], ns) == k, p, 0)
        return jnp.minimum(found, ns - 1)

    def send_rows(i):
        k = lax.rem(sp + 1 + i, ns)
        for j in range(nh):
            h = lax.rem(hd + j, nh)
            if i == ns - 1 and j == 0:
                recv[me] = send[i, h]
            else:
                pltpu.make_async_remote_copy(
                    src_ref=send.at[i, h],
                    dst_ref=recv.at[me],
                    send_sem=send_sem,
                    recv_sem=recv_sem,
                    device_id=(dp, h, k),
                    device_id_type=MESH,
                ).start()

    for chunk in range(ns // per):
        picked = [f_v[position(lax.rem(sp + 1 + chunk * per + t, ns))] for t in range(per)]
        values = jnp.concatenate(picked, axis=0).astype(jnp.float32)
        centred = values - jnp.mean(values, -1, keepdims=True)
        inverse = lax.rsqrt(jnp.mean(centred * centred, -1, keepdims=True) + 1e-06)
        unit = centred * inverse
        normed = (unit * gain + shift).astype(jnp.bfloat16)
        if chunk == 0:
            loads[1].wait()
        hidden = jnp.dot(normed, w_v[...], preferred_element_type=jnp.float32) + first_bias
        slopes = (second * gelu_slope(hidden)).astype(jnp.bfloat16)
        scaled = lax.dot_general(slopes, w_v[...], NT, preferred_element_type=jnp.float32) * gain
        patch = inverse * (
            scaled
            - jnp.mean(scaled, -1, keepdims=True)
            - unit * jnp.mean(scaled * unit, -1, keepdims=True)
        )
        if chunk == 0:
            loads[2].wait()
        pixels = lax.dot_general(
            patch.astype(jnp.bfloat16), e_v[...], NT, preferred_element_type=jnp.float32
        )
        for t in range(per):
            for h in range(nh):
                at = (t * nh + h) * STRIP
                send[chunk * per + t, h] = stack(pixels[at : at + STRIP]).astype(jnp.bfloat16)
        if chunk == 0:
            pl.semaphore_wait(barrier, group - 1 + (nd - 1) * ns)
        for t in range(per):
            send_rows(chunk * per + t)

    loads[3].wait()
    loads[4].wait()
    for side in range(2):
        strip_f[...] = strip_v[side].astype(jnp.float32).reshape(rows * 16, CH)
        colmsg[side] = strip_f[pl.ds(15 * side, rows, stride=16), :].astype(jnp.bfloat16)
    act_copies = []
    for d, (dh, ds) in enumerate(SIDES):
        if dh == 0:
            src, dst = act_mid.at[0, rows - 1 if ds > 0 else 0], rowland.at[d]
        elif ds == 0:
            src, dst = colmsg.at[1 if dh > 0 else 0], colland.at[d - 2]
        else:
            src = act_mid.at[0, rows - 1 if ds > 0 else 0, pl.ds(CH - 16 if dh > 0 else 0, 16)]
            dst = cornerland.at[d - 4]
        act_copies.append(
            pltpu.make_async_remote_copy(
                src_ref=src,
                dst_ref=dst,
                send_sem=asend_sem.at[d],
                recv_sem=arecv_sem.at[d],
                device_id=(dp, lax.rem(hd + dh + nh, nh), lax.rem(sp + ds + ns, ns)),
                device_id_type=MESH,
            )
        )
    for copy in act_copies:
        copy.start()

    def present(dh, ds):
        inside = jnp.bool_(True)
        if dh != 0:
            inside = jnp.logical_and(inside, hd != (0 if dh > 0 else nh - 1))
        if ds != 0:
            inside = jnp.logical_and(inside, sp != (0 if ds > 0 else ns - 1))
        return jnp.where(inside, 1.0, 0.0).astype(jnp.float32)

    for copy in act_copies:
        copy.wait()
    for d, (dh, ds) in enumerate(SIDES):
        there = present(dh, ds)
        if dh == 0:
            sdrow_out[d] = silu_slope(rowland[d].astype(jnp.float32)) * there
        elif ds == 0:
            sdcol_out[d - 2, pl.ds(16, rows), :] = (
                silu_slope(colland[d - 2].astype(jnp.float32)) * there
            )
        else:
            tile = silu_slope(cornerland[d - 4].astype(jnp.float32)) * there
            line = 15 if dh > 0 else 0
            sdcol_out[0 if dh > 0 else 1, pl.ds(15 if ds > 0 else 16 + rows, 1), :] = tile[
                line : line + 1
            ]

    wanted = []
    for s in range(ns):
        r = jnp.int32(0)
        for p in range(ns):
            entry = row_map[s * ns + p]
            r = r + jnp.where(lax.div(entry, ns) == sp, lax.rem(entry, ns), 0)
        wanted.append(r)
    loads[5].wait()
    everything = pltpu.make_async_copy(
        recv.at[pl.ds(0, group - 1)], recv.at[pl.ds(0, group - 1)], recv_sem
    )
    everything.wait()
    squares = jnp.zeros((16, HALF), jnp.float32)
    for r in range(ns):
        source = jnp.int32(0)
        for s in range(ns):
            source = source + jnp.where(wanted[s] == r, s, 0)
        source = jnp.minimum(source, ns - 1)
        summed = recv[source].astype(jnp.float32)
        for h in range(1, nh):
            summed = summed + recv[h * ns + source].astype(jnp.float32)
        squares = squares + summed * summed
        pm[pl.ds(8 * r, 8), :] = unstack(summed)
    squares = squares[:8] + squares[8:]
    sq1[hd] = squares[:, :128] + squares[:, 128:256] + squares[:, 256:]

    lines = jnp.zeros((8, P3), jnp.float32)
    for d, (dh, ds) in enumerate(SIDES):
        r = ns - 1 if ds > 0 else 0
        q = STRIP - 1 if dh > 0 else 0
        if dh == 0:
            message = pm[pl.ds(8 * r, 8), :]
        elif ds == 0:
            parts = [pm[pl.ds(8 * i + q, 1), :] for i in range(ns)]
            if ns < 8:
                parts.append(lines[: 8 - ns])
            message = jnp.concatenate(parts, axis=0)
        else:
            message = jnp.broadcast_to(pm[pl.ds(8 * r + q, 1), :], (8, P3))
        hmsg[d] = stack(message).astype(jnp.bfloat16)
    halo_copies = []
    for d, (dh, ds) in enumerate(SIDES):
        halo_copies.append(
            pltpu.make_async_remote_copy(
                src_ref=hmsg.at[d],
                dst_ref=hland.at[d],
                send_sem=hsend_sem.at[d],
                recv_sem=hrecv_sem.at[d],
                device_id=(dp, lax.rem(hd + dh + nh, nh), lax.rem(sp + ds + ns, ns)),
                device_id_type=MESH,
            )
        )
    for copy in halo_copies:
        copy.start()

    for j in range(1, nh):
        pltpu.make_async_remote_copy(
            src_ref=sq1.at[hd],
            dst_ref=sq1.at[hd],
            send_sem=q_sem.at[0],
            recv_sem=q_sem.at[1],
            device_id=(dp, lax.rem(hd + j, nh), sp),
            device_id_type=MESH,
        ).start()

    spread = jnp.dot(pm[...].astype(jnp.bfloat16), t_v[...], preferred_element_type=jnp.float32)
    for b in range(PATCH):
        for r in range(ns):
            x_out[r + 1, pl.ds(16 + b, 8, stride=16), :] = spread[
                8 * r : 8 * r + 8, 128 * b : 128 * b + 128
            ]

    seven = sq1.at[pl.ds(0, nh - 1)]
    pltpu.make_async_copy(seven, seven, q_sem.at[1]).wait()
    mine = dp * ns + sp
    sq2[mine] = jnp.sum(sq1[...], axis=0)
    for j in range(1, nd * ns):
        other = lax.rem(mine + j, nd * ns)
        pltpu.make_async_remote_copy(
            src_ref=sq2.at[mine],
            dst_ref=sq2.at[mine],
            send_sem=q_sem.at[2],
            recv_sem=q_sem.at[3],
            device_id=(lax.div(other, ns), hd, lax.rem(other, ns)),
            device_id_type=MESH,
        ).start()

    for copy in halo_copies:
        copy.wait()
    for d, (dh, ds) in enumerate(SIDES):
        hp[pl.ds(8 * d, 8), :] = unstack(hland[d].astype(jnp.float32) * present(dh, ds))
    spread = jnp.dot(hp[...].astype(jnp.bfloat16), t_v[...], preferred_element_type=jnp.float32)
    for d, (dh, ds) in enumerate(SIDES):
        r = 0 if ds > 0 else ns + 1
        if dh == 0:
            for b in range(PATCH):
                x_out[r, pl.ds(16 + b, 8, stride=16), :] = spread[
                    8 * d : 8 * d + 8, 128 * b : 128 * b + 128
                ]
            continue
        for b in (PATCH - 2, PATCH - 1) if dh > 0 else (0, 1):
            column = b if dh > 0 else 16 + CH + b
            if ds != 0:
                x_out[r, pl.ds(column, 1), :] = spread[8 * d : 8 * d + 1, 128 * b : 128 * b + 128]
                continue
            for i in range(ns):
                x_out[i + 1, pl.ds(column, 1), :] = spread[
                    8 * d + i : 8 * d + i + 1, 128 * b : 128 * b + 128
                ]

    rest = sq2.at[pl.ds(0, nd * ns - 1)]
    pltpu.make_async_copy(rest, rest, q_sem.at[3]).wait()
    total_out[...] = jnp.sum(sq2[...], axis=0)
    pltpu.make_async_copy(rest, rest, q_sem.at[2]).wait()
    pltpu.make_async_copy(seven, seven, q_sem.at[0]).wait()
    pltpu.make_async_copy(
        recv.at[pl.ds(0, group - 1)], recv.at[pl.ds(0, group - 1)], send_sem
    ).wait()


def decode_kernel(
    ns,
    entries,
    x_ref,
    sdrow,
    sdcol,
    total,
    taps,
    res,
    act_mid,
    act_in,
    out,
    mid_v,
    line_f,
    row_f,
    wr_v,
    am_v,
    ai_v,
    out_v,
    in_sem,
    out_sem,
):
    rows = ns * PATCH
    loads = []
    for i, (src, dst) in enumerate(((act_mid, am_v), (act_in, ai_v))):
        for g in range(ns):
            part = pl.ds(g * PATCH, PATCH)
            loads.append(pltpu.make_async_copy(src.at[0, part], dst.at[part], in_sem.at[i, g]))
    for load in loads:
        load.start()

    for i in range(4):
        for j in range(2):
            for b in range(3):
                a = i - j
                if 0 <= a <= 2:
                    block = res[2 - a, 2 - b]
                else:
                    block = jnp.zeros((CH, CH), jnp.bfloat16)
                wr_v[pl.ds(j * CH, CH), pl.ds((i * 3 + b) * CH, CH)] = block

    lane = lax.broadcasted_iota(jnp.int32, (PADC, 128), 1)

    def pairs(block, count):
        line_f[...] = jnp.where(lane < 6, pltpu.roll(x_ref[block], 80, 1), x_ref[block + 1])
        lhs = jnp.concatenate(
            [
                line_f[pl.ds(7, 144), :] + pltpu.roll(line_f[pl.ds(8, 144), :], 64, 1),
                line_f[pl.ds(9, 144), :],
            ],
            axis=1,
        ).astype(jnp.bfloat16)
        for t in range(count):
            band = jnp.concatenate(
                [taps[pl.ds(512 * t, 256), :], taps[pl.ds(512 * t + 256, 256), :]], axis=1
            )
            act = jnp.dot(lhs, band, preferred_element_type=jnp.float32)
            for i in range(2):
                slot = 2 * t + i
                r = block * PATCH + slot - 1
                grad = act[:, i * CH : (i + 1) * CH]
                if slot == 0:
                    slope = silu_slope(am_v[jnp.maximum(r, 0)].astype(jnp.float32))
                    slope = jnp.where(r < 0, sdrow[0], slope)
                elif count == 1:
                    slope = sdrow[1]
                else:
                    slope = silu_slope(am_v[r].astype(jnp.float32))
                row_f[slot, pl.ds(0, 8), :] = grad[:8] * sdcol[0, pl.ds(r + 16, 1), :]
                row_f[slot, pl.ds(8, CH), :] = grad[8 : 8 + CH] * slope
                row_f[slot, pl.ds(8 + CH, 8), :] = grad[8 + CH :] * sdcol[1, pl.ds(r + 16, 1), :]
                for b in range(3):
                    mid_v[block * 8 + t, :, pl.ds((i * 3 + b) * CH, CH)] = row_f[
                        slot, pl.ds(7 + b, CH), :
                    ].astype(jnp.bfloat16)

    for load in loads[:ns]:
        load.wait()

    def first(block, carry):
        pairs(block, 8)
        return carry

    lax.fori_loop(0, ns, first, 0)
    pairs(ns, 1)

    for load in loads[ns:]:
        load.wait()
    scale = lax.rsqrt(jnp.sum(total[...], keepdims=True) / entries + 1e-06)

    def second(g, carry):
        near = mid_v[pl.ds(8 * g, 8)].reshape(8 * CH, 6 * CH)
        far = mid_v[pl.ds(8 * g + 1, 8)].reshape(8 * CH, 6 * CH)
        spread = lax.dot_general(
            near, wr_v[:, pl.ds(0, 6 * CH)], NT, preferred_element_type=jnp.float32
        ) + lax.dot_general(
            far, wr_v[:, pl.ds(6 * CH, 6 * CH)], NT, preferred_element_type=jnp.float32
        )
        for q in range(8):
            for j in range(2):
                row = g * PATCH + 2 * q + j
                part = spread[q * CH : (q + 1) * CH, j * CH : (j + 1) * CH]
                mid = mid_v[8 * g + q + j, :, pl.ds((4 - 3 * j) * CH, CH)].astype(jnp.float32)
                slope = silu_slope(ai_v[row].astype(jnp.float32))
                out_v[row] = (scale * (mid + slope * part)).astype(jnp.bfloat16)
        part = pl.ds(g * PATCH, PATCH)
        pltpu.make_async_copy(out_v.at[part], out.at[0, part], out_sem).start()
        return carry

    lax.fori_loop(0, ns, second, 0)
    pltpu.make_async_copy(out_v, out.at[0], out_sem).wait()


def local(
    nd,
    nh,
    ns,
    features,
    row_map,
    head_weights,
    ln_gain,
    ln_bias,
    head_in,
    head_bias,
    head_out,
    patch_embed,
    act_in,
    act_mid,
    res_conv,
    out_conv,
):
    C = features.shape[-1]
    HID = head_in.shape[-1]
    rows = ns * PATCH
    group = nh * ns
    per = min(2, ns)
    f32, bf16 = jnp.float32, jnp.bfloat16
    vmem = pl.BlockSpec(memory_space=pltpu.VMEM)
    smem = pl.BlockSpec(memory_space=pltpu.SMEM)
    hbm = pl.BlockSpec(memory_space=pl.ANY)
    x, sdrow, sdcol, total = pl.pallas_call(
        functools.partial(trunk_kernel, nd, nh, ns, per),
        out_shape=(
            jax.ShapeDtypeStruct((ns + 2, PADC, 128), f32),
            jax.ShapeDtypeStruct((2, CH, CH), f32),
            jax.ShapeDtypeStruct((2, rows + 32, CH), f32),
            jax.ShapeDtypeStruct((8, 128), f32),
        ),
        in_specs=[smem, smem, hbm, vmem, vmem, hbm, vmem, vmem, hbm, hbm, hbm],
        out_specs=(vmem,) * 4,
        scratch_shapes=[
            pltpu.VMEM(features.shape[1:], bf16),
            pltpu.VMEM((C, HID), bf16),
            pltpu.VMEM((P3, C), bf16),
            pltpu.VMEM((P3, PATCH * 128), bf16),
            pltpu.VMEM((2, rows, 16, CH), bf16),
            pltpu.VMEM((rows * 16, CH), f32),
            pltpu.VMEM((ns, nh, 16, HALF), bf16),
            pltpu.VMEM((group, 16, HALF), bf16),
            pltpu.VMEM((2, rows, CH), bf16),
            pltpu.VMEM((2, CH, CH), bf16),
            pltpu.VMEM((2, rows, CH), bf16),
            pltpu.VMEM((4, 16, CH), bf16),
            pltpu.VMEM((8, 16, HALF), bf16),
            pltpu.VMEM((8, 16, HALF), bf16),
            pltpu.VMEM((8 * ns, P3), f32),
            pltpu.VMEM((64, P3), f32),
            pltpu.VMEM((nh, 8, 128), f32),
            pltpu.VMEM((nd * ns, 8, 128), f32),
            pltpu.SemaphoreType.DMA((6,)),
            pltpu.SemaphoreType.DMA,
            pltpu.SemaphoreType.DMA,
            pltpu.SemaphoreType.DMA((8,)),
            pltpu.SemaphoreType.DMA((8,)),
            pltpu.SemaphoreType.DMA((8,)),
            pltpu.SemaphoreType.DMA((8,)),
            pltpu.SemaphoreType.DMA((4,)),
        ],
        compiler_params=pltpu.CompilerParams(
            collective_id=0, has_side_effects=True, vmem_limit_bytes=48 * 1024 * 1024
        ),
    )(
        row_map,
        head_weights,
        features,
        ln_gain[None],
        ln_bias[None],
        head_in,
        head_bias,
        head_out,
        patch_embed,
        act_mid,
        jnp.asarray(spread_table(), bf16),
    )

    flat = out_conv[::-1, ::-1].transpose(0, 1, 3, 2).reshape(27, CH)
    taps = jnp.dot(
        jnp.asarray(tap_table(), bf16),
        jnp.pad(flat, ((0, 5), (0, 0))),
        preferred_element_type=f32,
    ).astype(bf16)
    return pl.pallas_call(
        functools.partial(decode_kernel, ns, float(nd * ns * ns * nh * STRIP * P3)),
        out_shape=jax.ShapeDtypeStruct(act_in.shape, bf16),
        in_specs=[vmem] * 6 + [hbm, hbm],
        out_specs=hbm,
        scratch_shapes=[
            pltpu.VMEM((8 * ns + 1, CH, 6 * CH), bf16),
            pltpu.VMEM((PADC, 128), f32),
            pltpu.VMEM((PATCH, 144, 128), f32),
            pltpu.VMEM((2 * CH, 12 * CH), bf16),
            pltpu.VMEM((rows, CH, CH), bf16),
            pltpu.VMEM((rows, CH, CH), bf16),
            pltpu.VMEM((rows, CH, CH), bf16),
            pltpu.SemaphoreType.DMA((2, ns)),
            pltpu.SemaphoreType.DMA,
        ],
        compiler_params=pltpu.CompilerParams(vmem_limit_bytes=56 * 1024 * 1024),
    )(x, sdrow, sdcol, total, taps, res_conv, act_mid, act_in)


def solution(mesh):
    nd, nh, ns = mesh.shape["dp"], mesh.shape["head"], mesh.shape["space"]
    in_specs = (
        P("dp", "space", None, None),
        P(),
        P("dp", "head"),
        P(),
        P(),
        P("head", None, None),
        P("head", None),
        P("head", None),
        P(),
        P("dp", "space", "head", None),
        P("dp", "space", "head", None),
        P(),
        P(),
    )
    out_specs = P("dp", "space", "head", None)
    return jax.shard_map(
        functools.partial(local, nd, nh, ns),
        mesh=mesh,
        in_specs=in_specs,
        out_specs=out_specs,
        check_vma=False,
    )
```

profile of v0, /device:TPU:1, one launch (start us, length us, event | category | flops | bytes accessed | tf_op | source)
XLA Modules:
  0.0 69.4 jit_solution(16330898167635201295)
XLA Ops:
  0.0 0.0 copy-start
  0.8 0.7 %broadcast_in_dim.6.gain_ref = f32[1,1280]{1,0:T(1,128)S(1)} reshape(f32[1280]{0:T(1024)} %param.18) | data formatting | bytes 10240 | tf_op jit(solution)/shard_map/broadcast_in_dim | solution.py:565
  1.5 0.7 %broadcast_in_dim.7.shift_ref = f32[1,1280]{1,0:T(1,128)S(1)} reshape(f32[1280]{0:T(1024)} %param.19) | data formatting | bytes 10240 | tf_op jit(solution)/shard_map/broadcast_in_dim | solution.py:566
  2.2 0.7 %reverse_bitcast_fusion = bf16[3,3,3,128]{3,2,1,0:T(4,128)(2,1)S(1)} fusion(bf16[3,3,128,3]{2,3,1,0:T(4,128)(2,1)} %param.27), kind=kLoop, calls=%fused_computation.2 | loop fusion | bytes 13824 | tf_op jit(solution)/shard_map/transpose | solution.py:575
  2.9 2.6 %fusion.taps = bf16[4096,128]{1,0:T(8,128)(2,1)} fusion(bf16[4096,32]{1,0:T(8,128)(2,1)} %constant.8.clone, bf16[27,128]{1,0:T(8,128)(2,1)S(1)} %reshape.3), kind=kOutput, calls=%fused_computation.1 | convolution fusion | flops 34078720 | bytes 1317632 | tf_op jit(solution)/shard_map/dot_general | solution.py:576
  5.5 0.0 copy-done
  5.5 0.0 copy-start.1
  5.5 1.3 %copy-done.1 = bf16[1,8,64,1280]{3,2,1,0:T(8,128)(2,1)S(1)} copy-done((bf16[1,8,64,1280]{3,2,1,0:T(8,128)(2,1)S(1)}, bf16[1,8,64,1280]{3,2,1,0:T(8,128)(2,1)}, u32[]{:S(2)}) %copy-start.1) | copy-done | bytes 1310744
  6.8 0.0 copy-start.5
  6.8 0.7 copy-done.5
  7.5 0.0 copy-start.6
  7.5 0.7 copy-done.6
  8.2 0.0 copy-start.8
  8.2 0.7 copy-done.8
  8.9 36.1 %shard_map.145 = (f32[10,160,128]{2,1,0:T(8,128)S(1)}, f32[2,128,128]{2,1,0:T(8,128)S(1)}, f32[2,160,128]{2,1,0:T(8,128)S(1)}, f32[8,128]{1,0:T(8,128)S(1)}) custom-call(s32[64]{0:T(128)S(1)} %copy-done.8, s32[1,1]{1,0:T(1,128)S(6)} %copy.18.weight, bf16[1,8,64,1280]{3,2,1,0:T(8,128)(2,1)S(1)} %copy-done.1, f32[1,1280]{1,0:T(1,128)S(1)} %broadcast_in_dim.6.gain_ref, ...), custom_call_target="tpu_custom_call" | custom-call | tf_op jit(solution)/shard_map/pallas_call | solution.py:520
  44.9 0.0 copy-start.2
  44.9 0.9 %copy-done.2 = f32[10,160,128]{2,1,0:T(8,128)} copy-done((f32[10,160,128]{2,1,0:T(8,128)}, f32[10,160,128]{2,1,0:T(8,128)S(1)}, u32[]{:S(2)}) %copy-start.2) | copy-done | bytes 819224
  45.9 0.0 copy-start.3
  45.9 0.7 copy-done.3
  46.5 0.0 copy-start.4
  46.5 0.6 copy-done.4
  47.2 0.0 copy-start.7
  47.2 0.6 copy-done.7
  47.8 21.7 %shard_map.146 = bf16[1,128,128,128]{3,2,1,0:T(8,128)(2,1)} custom-call(f32[10,160,128]{2,1,0:T(8,128)} %copy-done.2, f32[2,128,128]{2,1,0:T(8,128)} %copy-done.4, f32[2,160,128]{2,1,0:T(8,128)} %copy-done.3, f32[8,128]{1,0:T(8,128)} %copy-done.7, bf16[4096,128]{1,0:T(8,128)(2,1)} %fusion.taps, bf16[3,3,128,128]{3,2,1,0:T(8,128)(2,1)} %res.1, ...), custom_call_target="tpu_custom_call" | custom-call | tf_op jit(solution)/shard_map/pallas_call | solution.py:581
  (1 shorter events, 0.0 us)
Async XLA Ops:
  0.0 5.5 %copy-start = (bf16[768,1280]{1,0:T(8,128)(2,1)S(1)}, bf16[768,1280]{1,0:T(8,128)(2,1)}, u32[]{:S(2)}) copy-start(bf16[768,1280]{1,0:T(8,128)(2,1)} %e_hbm.1) | copy-start | bytes 5898244
  5.5 1.3 %copy-start.1 = (bf16[1,8,64,1280]{3,2,1,0:T(8,128)(2,1)S(1)}, bf16[1,8,64,1280]{3,2,1,0:T(8,128)(2,1)}, u32[]{:S(2)}) copy-start(bf16[1,8,64,1280]{3,2,1,0:T(8,128)(2,1)} %feats.1) | copy-start | bytes 3932164
  6.8 0.7 copy-start.5
  7.5 0.7 copy-start.6
  8.2 0.7 copy-start.8
  44.9 0.9 %copy-start.2 = (f32[10,160,128]{2,1,0:T(8,128)}, f32[10,160,128]{2,1,0:T(8,128)S(1)}, u32[]{:S(2)}) copy-start(f32[10,160,128]{2,1,0:T(8,128)S(1)} %get-tuple-element.9.x_ref) | copy-start | bytes 2457604
  45.9 0.7 copy-start.3
  46.5 0.7 copy-start.4
  47.2 0.6 copy-start.7
where the time goes:
time: 69.8 us; the launch traced here: 69.4 us
  Pallas kernels  57.7 us (83%)
  local copies, waits for them, and re-layouts  8.32 us (12%)
  matrix products  2.6 us (4%)
  between operations  0.82 us (1%)
    pallas_call x1, Pallas kernels, local(): pl.pallas_call(functools.partial(trunk_kernel, nd, nh, ns, per), out_shap...  36.1 us
    pallas_call x1, Pallas kernels, local(): pl.pallas_call(functools.partial(decode_kernel, ns, float(nd * ns * ns *...  21.7 us
    unnamed x18, local copies, waits for them, and re-layouts  6.19 us
    dot_general x1, matrix products, local(): jnp.dot(jnp.asarray(tap_table(), bf16), jnp.pad(flat, ((0, 5), (0, 0))),...  2.6 us

commit v1 on v0

v1 whole, which is shorter than its diff:
```python
import functools

import jax
import jax.numpy as jnp
from jax import lax
from jax.experimental import pallas as pl
from jax.experimental.pallas import tpu as pltpu
from jax.sharding import PartitionSpec as P

MESH = pl.DeviceIdType.MESH
PATCH = 16
P3 = 768
HALF = 384
CH = 128
STRIP = 8
PADC = 160
NT = (((1,), (1,)), ((), ()))
SIDES = ((0, 1), (0, -1), (1, 0), (-1, 0), (1, 1), (-1, 1), (1, -1), (-1, -1))


def gelu_slope(v):
    bell = jnp.exp(-0.5 * v * v)
    t = 1.0 / (1.0 + 0.2316418882663604 * jnp.abs(v))
    poly = t * (
        0.127414796
        + t * (-0.142248368 + t * (0.7107068705 + t * (-0.7265760135 + t * 0.5307027145)))
    )
    tail = poly * bell
    return jnp.where(v >= 0, 1.0 - tail, tail) + v * bell * 0.3989422804014327


def silu_slope(v):
    half = 0.5 * v.astype(jnp.float32)
    t = jnp.tanh(half)
    return (0.5 + 0.5 * t) * (1.0 + half * (1.0 - t))


def stack(values):
    return jnp.concatenate([values[:, :HALF], values[:, HALF:]], axis=0)


def unstack(values):
    return jnp.concatenate([values[:8], values[8:]], axis=1)


def trunk_kernel(
    nd,
    nh,
    ns,
    order,
    per,
    weight,
    map_hbm,
    feats,
    gain_hbm,
    shift_hbm,
    w_hbm,
    hb_hbm,
    ho_hbm,
    e_hbm,
    act_in,
    act_mid,
    res_hbm,
    tap_hbm,
    mid_out,
    slope_out,
    wr_out,
    total_out,
    row_map,
    f_v,
    w_v,
    e_v,
    t_v,
    g_v,
    b_v,
    hb_v,
    ho_v,
    res_v,
    tap_v,
    band_f,
    band_v,
    am_v,
    normed_v,
    unit_v,
    strip_v,
    strip_f,
    send,
    recv,
    colmsg,
    rowland,
    colland,
    cornerland,
    sdrow,
    sdcol,
    hmsg,
    hland,
    pm,
    hp,
    x_v,
    line_f,
    row_f,
    sq1,
    sq2,
    load_sem,
    act_sem,
    send_sem,
    recv_sem,
    asend_sem,
    arecv_sem,
    hsend_sem,
    hrecv_sem,
    q_sem,
):
    dp, hd, sp = lax.axis_index("dp"), lax.axis_index("head"), lax.axis_index("space")
    rows = ns * PATCH
    group = nh * ns
    me = hd * ns + sp
    barrier = pltpu.get_barrier_semaphore()

    def load(src, dst, i):
        return pltpu.make_async_copy(src, dst, load_sem.at[i])

    load_map = load(map_hbm, row_map, 0)
    load_f = load(feats.at[0], f_v, 1)
    load_g = load(gain_hbm, g_v, 2)
    load_b = load(shift_hbm, b_v, 3)
    load_w = load(w_hbm.at[0], w_v, 4)
    load_hb = load(hb_hbm, hb_v, 5)
    load_ho = load(ho_hbm, ho_v, 6)
    load_e = load(e_hbm, e_v, 7)
    load_near = load(act_mid.at[0, :, pl.ds(0, 16)], strip_v.at[0], 8)
    load_far = load(act_mid.at[0, :, pl.ds(CH - 16, 16)], strip_v.at[1], 9)
    load_res = load(res_hbm, res_v, 10)
    load_tap = load(tap_hbm, tap_v, 11)
    load_mid = pltpu.make_async_copy(act_mid.at[0], am_v, act_sem.at[0])
    load_in = pltpu.make_async_copy(act_in.at[0], slope_out, act_sem.at[1])
    for one in (load_map, load_f, load_g, load_b, load_w, load_hb, load_ho, load_e):
        one.start()

    def greet(i, carry):
        j = lax.rem(me + i, group)
        pl.semaphore_signal(
            barrier, inc=1, device_id=(dp, lax.div(j, ns), lax.rem(j, ns)), device_id_type=MESH
        )
        return carry

    lax.fori_loop(1, group, greet, 0)

    def greet_far(i, carry):
        pl.semaphore_signal(
            barrier,
            inc=1,
            device_id=(lax.rem(dp + 1 + lax.div(i, ns), nd), hd, lax.rem(i, ns)),
            device_id_type=MESH,
        )
        return carry

    lax.fori_loop(0, (nd - 1) * ns, greet_far, 0)

    load_map.wait()
    load_g.wait()
    load_b.wait()
    load_f.wait()
    gain = g_v[...].reshape(1, -1)
    shift = b_v[...].reshape(1, -1)
    cols = nh * STRIP

    def position(k):
        found = jnp.int32(0)
        for p in range(ns):
            found = found + jnp.where(lax.div(row_map[sp * ns + p], ns) == k, p, 0)
        return jnp.minimum(found, ns - 1)

    inverses = []
    for i, step in enumerate(order):
        values = f_v[position(lax.rem(sp + step, ns))].astype(jnp.float32)
        centred = values - jnp.mean(values, -1, keepdims=True)
        inverse = lax.rsqrt(jnp.mean(centred * centred, -1, keepdims=True) + 1e-06)
        unit = centred * inverse
        unit_v[pl.ds(i * cols, cols), :] = unit
        normed_v[pl.ds(i * cols, cols), :] = (unit * gain + shift).astype(jnp.bfloat16)
        inverses.append(inverse)

    load_hb.wait()
    load_ho.wait()
    second = ho_v[...] * weight[0, 0].astype(jnp.float32)
    first_bias = hb_v[...]
    load_w.wait()

    def send_rows(i):
        k = lax.rem(sp + order[i], ns)
        for j in range(nh):
            h = lax.rem(hd + j, nh)
            if order[i] == 0 and j == 0:
                recv[me] = send[i, h]
            else:
                pltpu.make_async_remote_copy(
                    src_ref=send.at[i, h],
                    dst_ref=recv.at[me],
                    send_sem=send_sem,
                    recv_sem=recv_sem,
                    device_id=(dp, h, k),
                    device_id_type=MESH,
                ).start()

    for chunk in range(ns // per):
        part = pl.ds(chunk * per * cols, per * cols)
        hidden = (
            jnp.dot(normed_v[part, :], w_v[...], preferred_element_type=jnp.float32) + first_bias
        )
        slopes = (second * gelu_slope(hidden)).astype(jnp.bfloat16)
        scaled = lax.dot_general(slopes, w_v[...], NT, preferred_element_type=jnp.float32) * gain
        unit = unit_v[part, :]
        inverse = jnp.concatenate(inverses[chunk * per : chunk * per + per], axis=0)
        patch = inverse * (
            scaled
            - jnp.mean(scaled, -1, keepdims=True)
            - unit * jnp.mean(scaled * unit, -1, keepdims=True)
        )
        if chunk == 0:
            load_e.wait()
            for one in (load_near, load_far, load_res, load_tap):
                one.start()
            load_mid.start()
            load_in.start()
        pixels = lax.dot_general(
            patch.astype(jnp.bfloat16), e_v[...], NT, preferred_element_type=jnp.float32
        )
        for t in range(per):
            for h in range(nh):
                at = (t * nh + h) * STRIP
                send[chunk * per + t, h] = stack(pixels[at : at + STRIP]).astype(jnp.bfloat16)
        if chunk == 0:
            pl.semaphore_wait(barrier, group - 1 + (nd - 1) * ns)
        for t in range(per):
            send_rows(chunk * per + t)

    load_near.wait()
    load_far.wait()
    for side in range(2):
        strip_f[...] = strip_v[side].astype(jnp.float32).reshape(rows * 16, CH)
        colmsg[side] = strip_f[pl.ds(15 * side, rows, stride=16), :].astype(jnp.bfloat16)
    act_copies = []
    for d, (dh, ds) in enumerate(SIDES):
        if dh == 0:
            src, dst = act_mid.at[0, rows - 1 if ds > 0 else 0], rowland.at[d]
        elif ds == 0:
            src, dst = colmsg.at[1 if dh > 0 else 0], colland.at[d - 2]
        else:
            src = act_mid.at[0, rows - 1 if ds > 0 else 0, pl.ds(CH - 16 if dh > 0 else 0, 16)]
            dst = cornerland.at[d - 4]
        act_copies.append(
            pltpu.make_async_remote_copy(
                src_ref=src,
                dst_ref=dst,
                send_sem=asend_sem.at[d],
                recv_sem=arecv_sem.at[d],
                device_id=(dp, lax.rem(hd + dh + nh, nh), lax.rem(sp + ds + ns, ns)),
                device_id_type=MESH,
            )
        )
    for copy in act_copies:
        copy.start()

    def present(dh, ds):
        inside = jnp.bool_(True)
        if dh != 0:
            inside = jnp.logical_and(inside, hd != (0 if dh > 0 else nh - 1))
        if ds != 0:
            inside = jnp.logical_and(inside, sp != (0 if ds > 0 else ns - 1))
        return jnp.where(inside, 1.0, 0.0).astype(jnp.float32)

    load_mid.wait()

    def slope_mid(i, carry):
        am_v[pl.ds(4 * i, 4)] = silu_slope(am_v[pl.ds(4 * i, 4)]).astype(jnp.bfloat16)
        return carry

    lax.fori_loop(0, rows // 4, slope_mid, 0)
    load_in.wait()

    def slope_in(i, carry):
        slope_out[pl.ds(4 * i, 4)] = silu_slope(slope_out[pl.ds(4 * i, 4)]).astype(jnp.bfloat16)
        return carry

    lax.fori_loop(0, rows // 4, slope_in, 0)

    line = lax.broadcasted_iota(jnp.int32, (256, 128), 0)
    goal = lax.rem(line, 16) * 64 + 6 + 3 * lax.div(line, 16)
    goal = goal - lax.broadcasted_iota(jnp.int32, (256, 128), 1)
    for o in range(3):
        for i in range(8):
            t_v[pl.ds(256 * o, 256), pl.ds(128 * i, 128)] = jnp.where(
                goal == 128 * i - o, 1.0, 0.0
            ).astype(jnp.bfloat16)

    load_tap.wait()
    load_res.wait()
    band_f[...] = jnp.zeros(band_f.shape, jnp.float32)
    for a in range(3):
        for b in range(3):
            band_f[pl.ds(48 + 64 * b + 3 * a, 3), :] = tap_v[2 - a, 2 - b].astype(jnp.float32)
    for i in range(PATCH):
        band_v[i] = band_f[pl.ds(48 - 3 * i, 256), :].astype(jnp.bfloat16)
    for i in range(4):
        for j in range(2):
            for b in range(3):
                a = i - j
                if 0 <= a <= 2:
                    block = res_v[2 - a, 2 - b]
                else:
                    block = jnp.zeros((CH, CH), jnp.bfloat16)
                wr_out[pl.ds(j * CH, CH), pl.ds((i * 3 + b) * CH, CH)] = block

    for copy in act_copies:
        copy.wait()
    for d, (dh, ds) in enumerate(SIDES):
        there = present(dh, ds)
        if dh == 0:
            sdrow[d] = silu_slope(rowland[d]) * there
        elif ds == 0:
            sdcol[d - 2, pl.ds(16, rows), :] = silu_slope(colland[d - 2]) * there
        else:
            tile = silu_slope(cornerland[d - 4]) * there
            line = 15 if dh > 0 else 0
            sdcol[0 if dh > 0 else 1, pl.ds(15 if ds > 0 else 16 + rows, 1), :] = tile[
                line : line + 1
            ]

    wanted = []
    for s in range(ns):
        r = jnp.int32(0)
        for p in range(ns):
            entry = row_map[s * ns + p]
            r = r + jnp.where(lax.div(entry, ns) == sp, lax.rem(entry, ns), 0)
        wanted.append(r)
    everything = pltpu.make_async_copy(
        recv.at[pl.ds(0, group - 1)], recv.at[pl.ds(0, group - 1)], recv_sem
    )
    everything.wait()
    squares = jnp.zeros((16, HALF), jnp.float32)
    for r in range(ns):
        source = jnp.int32(0)
        for s in range(ns):
            source = source + jnp.where(wanted[s] == r, s, 0)
        source = jnp.minimum(source, ns - 1)
        summed = recv[source].astype(jnp.float32)
        for h in range(1, nh):
            summed = summed + recv[h * ns + source].astype(jnp.float32)
        squares = squares + summed * summed
        pm[pl.ds(8 * r, 8), :] = unstack(summed)

    lines = jnp.zeros((8, P3), jnp.float32)
    for d, (dh, ds) in enumerate(SIDES):
        r = ns - 1 if ds > 0 else 0
        q = STRIP - 1 if dh > 0 else 0
        if dh == 0:
            message = pm[pl.ds(8 * r, 8), :]
        elif ds == 0:
            parts = [pm[pl.ds(8 * i + q, 1), :] for i in range(ns)]
            if ns < 8:
                parts.append(lines[: 8 - ns])
            message = jnp.concatenate(parts, axis=0)
        else:
            message = jnp.broadcast_to(pm[pl.ds(8 * r + q, 1), :], (8, P3))
        hmsg[d] = stack(message).astype(jnp.bfloat16)
    halo_copies = []
    for d, (dh, ds) in enumerate(SIDES):
        halo_copies.append(
            pltpu.make_async_remote_copy(
                src_ref=hmsg.at[d],
                dst_ref=hland.at[d],
                send_sem=hsend_sem.at[d],
                recv_sem=hrecv_sem.at[d],
                device_id=(dp, lax.rem(hd + dh + nh, nh), lax.rem(sp + ds + ns, ns)),
                device_id_type=MESH,
            )
        )
    for copy in halo_copies:
        copy.start()

    squares = squares[:8] + squares[8:]
    sq1[hd] = squares[:, :128] + squares[:, 128:256] + squares[:, 256:]
    for j in range(1, nh):
        pltpu.make_async_remote_copy(
            src_ref=sq1.at[hd],
            dst_ref=sq1.at[hd],
            send_sem=q_sem.at[0],
            recv_sem=q_sem.at[1],
            device_id=(dp, lax.rem(hd + j, nh), sp),
            device_id_type=MESH,
        ).start()

    low = lax.broadcasted_iota(jnp.int32, (8, 128), 1) < 64

    def lanes_of(spread, at, b):
        tile = spread[at : at + 8, 128 * (b // 2) : 128 * (b // 2) + 128]
        if b % 2:
            tile = pltpu.roll(tile, 64, 1)
        return jnp.where(low, tile, 0.0)

    spread = jnp.dot(pm[...].astype(jnp.bfloat16), t_v[...], preferred_element_type=jnp.float32)
    for b in range(PATCH):
        for r in range(ns):
            x_v[r + 1, pl.ds(16 + b, 8, stride=16), :] = lanes_of(spread, 8 * r, b)

    for copy in halo_copies:
        copy.wait()
    for d, (dh, ds) in enumerate(SIDES):
        hp[pl.ds(8 * d, 8), :] = unstack(hland[d].astype(jnp.float32) * present(dh, ds))
    spread = jnp.dot(hp[...].astype(jnp.bfloat16), t_v[...], preferred_element_type=jnp.float32)
    for d, (dh, ds) in enumerate(SIDES):
        r = 0 if ds > 0 else ns + 1
        if dh == 0:
            for b in range(PATCH):
                x_v[r, pl.ds(16 + b, 8, stride=16), :] = lanes_of(spread, 8 * d, b)
            continue
        for b in (PATCH - 2, PATCH - 1) if dh > 0 else (0, 1):
            column = b if dh > 0 else 16 + CH + b
            tile = lanes_of(spread, 8 * d, b)
            if ds != 0:
                x_v[r, pl.ds(column, 1), :] = tile[:1]
                continue
            for i in range(ns):
                x_v[i + 1, pl.ds(column, 1), :] = tile[i : i + 1]

    seven = sq1.at[pl.ds(0, nh - 1)]
    pltpu.make_async_copy(seven, seven, q_sem.at[1]).wait()
    mine = dp * ns + sp
    sq2[mine] = jnp.sum(sq1[...], axis=0)
    for j in range(1, nd * ns):
        other = lax.rem(mine + j, nd * ns)
        pltpu.make_async_remote_copy(
            src_ref=sq2.at[mine],
            dst_ref=sq2.at[mine],
            send_sem=q_sem.at[2],
            recv_sem=q_sem.at[3],
            device_id=(lax.div(other, ns), hd, lax.rem(other, ns)),
            device_id_type=MESH,
        ).start()

    lane = lax.broadcasted_iota(jnp.int32, (PADC, 128), 1)

    def left_side(block, u):
        line_f[u] = jnp.where(lane < 6, pltpu.roll(x_v[block], 80, 1), x_v[block + 1])
        return jnp.concatenate(
            [
                line_f[u, pl.ds(7, 144), :] + pltpu.roll(line_f[u, pl.ds(8, 144), :], 64, 1),
                line_f[u, pl.ds(9, 144), :],
            ],
            axis=1,
        ).astype(jnp.bfloat16)

    def pairs(block, blocks, count):
        lhs = jnp.concatenate([left_side(block + u, u) for u in range(blocks)], axis=0)
        for t in range(count):
            band = jnp.concatenate([band_v[2 * t], band_v[2 * t + 1]], axis=1)
            act = jnp.dot(lhs, band, preferred_element_type=jnp.float32)
            for u in range(blocks):
                for i in range(2):
                    slot = 2 * t + i
                    r = (block + u) * PATCH + slot - 1
                    grad = act[144 * u : 144 * u + 144, i * CH : (i + 1) * CH]
                    if slot == 0 and u == 0 and count > 1:
                        slope = am_v[jnp.maximum(r, 0)].astype(jnp.float32)
                        slope = jnp.where(r < 0, sdrow[0], slope)
                    elif slot == 1 and count == 1:
                        slope = sdrow[1]
                    else:
                        slope = am_v[r].astype(jnp.float32)
                    spot = u * PATCH + slot
                    row_f[spot, pl.ds(0, 8), :] = grad[:8] * sdcol[0, pl.ds(r + 16, 1), :]
                    row_f[spot, pl.ds(8, CH), :] = grad[8 : 8 + CH] * slope
                    row_f[spot, pl.ds(8 + CH, 8), :] = (
                        grad[8 + CH :] * sdcol[1, pl.ds(r + 16, 1), :]
                    )
                    for b in range(3):
                        mid_out[(block + u) * 8 + t, :, pl.ds((i * 3 + b) * CH, CH)] = row_f[
                            spot, pl.ds(7 + b, CH), :
                        ].astype(jnp.bfloat16)

    def first(block, carry):
        pairs(2 * block, 2, 8)
        return carry

    lax.fori_loop(0, ns // 2, first, 0)
    pairs(ns, 1, 1)

    rest = sq2.at[pl.ds(0, nd * ns - 1)]
    pltpu.make_async_copy(rest, rest, q_sem.at[3]).wait()
    total_out[...] = jnp.sum(sq2[...], axis=0)
    pltpu.make_async_copy(rest, rest, q_sem.at[2]).wait()
    pltpu.make_async_copy(seven, seven, q_sem.at[0]).wait()
    pltpu.make_async_copy(
        recv.at[pl.ds(0, group - 1)], recv.at[pl.ds(0, group - 1)], send_sem
    ).wait()


def decode_kernel(ns, entries, mid_ref, slope_ref, wr_ref, total, out, out_v, out_sem):
    scale = lax.rsqrt(jnp.sum(total[...], keepdims=True) / entries + 1e-06)

    def second(g, carry):
        near = mid_ref[pl.ds(8 * g, 8)].reshape(8 * CH, 6 * CH)
        far = mid_ref[pl.ds(8 * g + 1, 8)].reshape(8 * CH, 6 * CH)
        spread = lax.dot_general(
            near, wr_ref[:, pl.ds(0, 6 * CH)], NT, preferred_element_type=jnp.float32
        ) + lax.dot_general(
            far, wr_ref[:, pl.ds(6 * CH, 6 * CH)], NT, preferred_element_type=jnp.float32
        )
        for q in range(8):
            for j in range(2):
                row = g * PATCH + 2 * q + j
                part = spread[q * CH : (q + 1) * CH, j * CH : (j + 1) * CH]
                mid = mid_ref[8 * g + q + j, :, pl.ds((4 - 3 * j) * CH, CH)].astype(jnp.float32)
                slope = slope_ref[row].astype(jnp.float32)
                out_v[row] = (scale * (mid + slope * part)).astype(jnp.bfloat16)
        part = pl.ds(g * PATCH, PATCH)
        pltpu.make_async_copy(out_v.at[part], out.at[0, part], out_sem).start()
        return carry

    lax.fori_loop(0, ns, second, 0)
    pltpu.make_async_copy(out_v, out.at[0], out_sem).wait()


def local(
    nd,
    nh,
    ns,
    features,
    row_map,
    head_weights,
    ln_gain,
    ln_bias,
    head_in,
    head_bias,
    head_out,
    patch_embed,
    act_in,
    act_mid,
    res_conv,
    out_conv,
):
    C = features.shape[-1]
    HID = head_in.shape[-1]
    rows = ns * PATCH
    group = nh * ns
    patches = ns * nh * STRIP
    order = [s % ns for s in (2, -2, 3, -3, 4, 1, -1)]
    order = [s for i, s in enumerate(order) if s and s not in order[:i]] + [0]
    per = max(1, ns // 2)
    f32, bf16 = jnp.float32, jnp.bfloat16
    vmem = pl.BlockSpec(memory_space=pltpu.VMEM)
    smem = pl.BlockSpec(memory_space=pltpu.SMEM)
    hbm = pl.BlockSpec(memory_space=pl.ANY)
    dma = pltpu.SemaphoreType.DMA
    mid, slope, wr, total = pl.pallas_call(
        functools.partial(trunk_kernel, nd, nh, ns, order, per),
        out_shape=(
            pltpu.VMEM((8 * ns + 1, CH, 6 * CH), bf16),
            pltpu.VMEM((rows, CH, CH), bf16),
            pltpu.VMEM((2 * CH, 12 * CH), bf16),
            pltpu.VMEM((8, 128), f32),
        ),
        in_specs=[smem] + [pl.BlockSpec(memory_space=pltpu.HBM)] * 12,
        out_specs=(vmem,) * 4,
        scratch_shapes=[
            pltpu.SMEM(row_map.shape, jnp.int32),
            pltpu.VMEM(features.shape[1:], bf16),
            pltpu.VMEM((C, HID), bf16),
            pltpu.VMEM((P3, C), bf16),
            pltpu.VMEM((P3, PATCH * 64), bf16),
            pltpu.VMEM((C,), f32),
            pltpu.VMEM((C,), f32),
            pltpu.VMEM((1, HID), f32),
            pltpu.VMEM((1, HID), f32),
            pltpu.VMEM(res_conv.shape, bf16),
            pltpu.VMEM((3, 3, 3, CH), bf16),
            pltpu.VMEM((304, CH), f32),
            pltpu.VMEM((PATCH, 256, CH), bf16),
            pltpu.VMEM((rows, CH, CH), bf16),
            pltpu.VMEM((patches, C), bf16),
            pltpu.VMEM((patches, C), f32),
            pltpu.VMEM((2, rows, 16, CH), bf16),
            pltpu.VMEM((rows * 16, CH), f32),
            pltpu.VMEM((ns, nh, 16, HALF), bf16),
            pltpu.VMEM((group, 16, HALF), bf16),
            pltpu.VMEM((2, rows, CH), bf16),
            pltpu.VMEM((2, CH, CH), bf16),
            pltpu.VMEM((2, rows, CH), bf16),
            pltpu.VMEM((4, 16, CH), bf16),
            pltpu.VMEM((2, CH, CH), f32),
            pltpu.VMEM((2, rows + 32, CH), f32),
            pltpu.VMEM((8, 16, HALF), bf16),
            pltpu.VMEM((8, 16, HALF), bf16),
            pltpu.VMEM((8 * ns, P3), f32),
            pltpu.VMEM((64, P3), f32),
            pltpu.VMEM((ns + 2, PADC, 128), f32),
            pltpu.VMEM((2, PADC, 128), f32),
            pltpu.VMEM((2 * PATCH, 144, 128), f32),
            pltpu.VMEM((nh, 8, 128), f32),
            pltpu.VMEM((nd * ns, 8, 128), f32),
            dma((12,)),
            dma((2,)),
            dma,
            dma,
            dma((8,)),
            dma((8,)),
            dma((8,)),
            dma((8,)),
            dma((4,)),
        ],
        compiler_params=pltpu.CompilerParams(
            collective_id=0, has_side_effects=True, vmem_limit_bytes=40 * 1024 * 1024
        ),
    )(
        head_weights,
        row_map,
        features,
        ln_gain,
        ln_bias,
        head_in,
        head_bias,
        head_out,
        patch_embed,
        act_in,
        act_mid,
        res_conv,
        out_conv.transpose(0, 1, 3, 2),
    )
    return pl.pallas_call(
        functools.partial(decode_kernel, ns, float(nd * ns * ns * nh * STRIP * P3)),
        out_shape=jax.ShapeDtypeStruct(act_in.shape, bf16),
        in_specs=[vmem] * 4,
        out_specs=hbm,
        scratch_shapes=[pltpu.VMEM((rows, CH, CH), bf16), dma],
        compiler_params=pltpu.CompilerParams(vmem_limit_bytes=16 * 1024 * 1024),
    )(mid, slope, wr, total)


def solution(mesh):
    nd, nh, ns = mesh.shape["dp"], mesh.shape["head"], mesh.shape["space"]
    in_specs = (
        P("dp", "space", None, None),
        P(),
        P("dp", "head"),
        P(),
        P(),
        P("head", None, None),
        P("head", None),
        P("head", None),
        P(),
        P("dp", "space", "head", None),
        P("dp", "space", "head", None),
        P(),
        P(),
    )
    out_specs = P("dp", "space", "head", None)
    return jax.shard_map(
        functools.partial(local, nd, nh, ns),
        mesh=mesh,
        in_specs=in_specs,
        out_specs=out_specs,
        check_vma=False,
    )
```

time: 69.8 us -> 44.7 us (0.64)
  Pallas kernels: 57.7 us -> 43.9 us
  local copies, waits for them, and re-layouts: 8.32 us -> 0 us
  matrix products: 2.6 us -> 0 us
    pallas_call x1, Pallas kernels: 21.7 us -> 9.04 us  [local(): pl.pallas_call(functools.partial(decode_kernel, ns, float(nd * ns * ns *...]
    unnamed x18 -> x0, local copies, waits for them, and re-layouts: 6.19 us -> none
    dot_general x1 -> x0, matrix products: 2.6 us -> none  [local(): jnp.dot(jnp.asarray(tap_table(), bf16), jnp.pad(flat, ((0, 5), (0, 0))),...]
    broadcast_in_dim x2 -> x0, local copies, waits for them, and re-layouts: 1.4 us -> none  [the longest x1 0.7 us: local(): ln_gain[None]]
    pallas_call x1, Pallas kernels: 36.1 us -> 34.9 us  [local(): pl.pallas_call(functools.partial(trunk_kernel, nd, nh, ns, order, per), o...]
    transpose x1 -> x0, local copies, waits for them, and re-layouts: 0.7 us -> none  [local(): flat = out_conv[::-1, ::-1].transpose(0, 1, 3, 2).reshape(27, CH)]
where the time goes in v1:
time: 44.7 us; the launch traced here: 44.6 us
  Pallas kernels  43.9 us (98%)
  between operations  0.66 us (1%)
    pallas_call x1, Pallas kernels, local(): pl.pallas_call(functools.partial(trunk_kernel, nd, nh, ns, order, per), o...  34.9 us
    pallas_call x1, Pallas kernels, local(): pl.pallas_call(functools.partial(decode_kernel, ns, float(nd * ns * ns *...  9.04 us

profile of v1, /device:TPU:1, one launch (start us, length us, event | category | flops | bytes accessed | tf_op | source)
XLA Modules:
  0.0 44.6 jit_solution(1329960445504453113)
XLA Ops:
  0.7 34.9 %shard_map.127 = (bf16[65,128,768]{2,1,0:T(8,128)(2,1)S(1)}, bf16[128,128,128]{2,1,0:T(8,128)(2,1)S(1)}, bf16[256,1536]{1,0:T(8,128)(2,1)S(1)}, f32[8,128]{1,0:T(8,128)S(1)}) custom-call(s32[1,1]{1,0:T(1,128)S(6)} %copy.14.weight, s32[64]{0:T(128)} %map_hbm.1, bf16[1,8,64,1280]{3,2,1,0:T(8,128)(2,1)} %feats.1, f32[1280]{0:T(1024)} %gain_hbm.1, ...), custom_call_target="tpu_custom_call" | custom-call | tf_op jit(solution)/shard_map/pallas_call | solution.py:556
  35.6 9.0 %shard_map.128 = bf16[1,128,128,128]{3,2,1,0:T(8,128)(2,1)} custom-call(bf16[65,128,768]{2,1,0:T(8,128)(2,1)S(1)} %get-tuple-element.9.mid_ref, bf16[128,128,128]{2,1,0:T(8,128)(2,1)S(1)} %get-tuple-element.10.slope_ref, bf16[256,1536]{1,0:T(8,128)(2,1)S(1)} %get-tuple-element.11.wr_ref, f32[8,128]{1,0:T(8,128)S(1)} %get-tuple-element.12.total), custom_call_target="tpu_custom_call" | custom-call | tf_op jit(solution)/shard_map/pallas_call | solution.py:630

commit v2 on v1

--- a/solution.py
+++ b/solution.py
@@ -82,7 +82,6 @@
     am_v,
     normed_v,
     unit_v,
-    strip_v,
     strip_f,
     send,
     recv,
@@ -99,6 +98,8 @@
     x_v,
     line_f,
     row_f,
+    edge_v,
+    fix_f,
     sq1,
     sq2,
     load_sem,
@@ -128,10 +129,8 @@
     load_hb = load(hb_hbm, hb_v, 5)
     load_ho = load(ho_hbm, ho_v, 6)
     load_e = load(e_hbm, e_v, 7)
-    load_near = load(act_mid.at[0, :, pl.ds(0, 16)], strip_v.at[0], 8)
-    load_far = load(act_mid.at[0, :, pl.ds(CH - 16, 16)], strip_v.at[1], 9)
-    load_res = load(res_hbm, res_v, 10)
-    load_tap = load(tap_hbm, tap_v, 11)
+    load_res = load(res_hbm, res_v, 8)
+    load_tap = load(tap_hbm, tap_v, 9)
     load_mid = pltpu.make_async_copy(act_mid.at[0], am_v, act_sem.at[0])
     load_in = pltpu.make_async_copy(act_in.at[0], slope_out, act_sem.at[1])
     for one in (load_map, load_f, load_g, load_b, load_w, load_hb, load_ho, load_e):
@@ -219,7 +218,7 @@
         )
         if chunk == 0:
             load_e.wait()
-            for one in (load_near, load_far, load_res, load_tap):
+            for one in (load_res, load_tap):
                 one.start()
             load_mid.start()
             load_in.start()
@@ -235,33 +234,6 @@
         for t in range(per):
             send_rows(chunk * per + t)
 
-    load_near.wait()
-    load_far.wait()
-    for side in range(2):
-        strip_f[...] = strip_v[side].astype(jnp.float32).reshape(rows * 16, CH)
-        colmsg[side] = strip_f[pl.ds(15 * side, rows, stride=16), :].astype(jnp.bfloat16)
-    act_copies = []
-    for d, (dh, ds) in enumerate(SIDES):
-        if dh == 0:
-            src, dst = act_mid.at[0, rows - 1 if ds > 0 else 0], rowland.at[d]
-        elif ds == 0:
-            src, dst = colmsg.at[1 if dh > 0 else 0], colland.at[d - 2]
-        else:
-            src = act_mid.at[0, rows - 1 if ds > 0 else 0, pl.ds(CH - 16 if dh > 0 else 0, 16)]
-            dst = cornerland.at[d - 4]
-        act_copies.append(
-            pltpu.make_async_remote_copy(
-                src_ref=src,
-                dst_ref=dst,
-                send_sem=asend_sem.at[d],
-                recv_sem=arecv_sem.at[d],
-                device_id=(dp, lax.rem(hd + dh + nh, nh), lax.rem(sp + ds + ns, ns)),
-                device_id_type=MESH,
-            )
-        )
-    for copy in act_copies:
-        copy.start()
-
     def present(dh, ds):
         inside = jnp.bool_(True)
         if dh != 0:
@@ -277,6 +249,10 @@
         return carry
 
     lax.fori_loop(0, rows // 4, slope_mid, 0)
+    for side in range(2):
+        edge = am_v[:, pl.ds((CH - 16) * side, 16), :].astype(jnp.float32)
+        strip_f[...] = edge.reshape(rows * 16, CH)
+        colmsg[side] = strip_f[pl.ds(15 * side, rows, stride=16), :].astype(jnp.bfloat16)
     load_in.wait()
 
     def slope_in(i, carry):
@@ -307,25 +283,10 @@
             for b in range(3):
                 a = i - j
                 if 0 <= a <= 2:
-                    block = res_v[2 - a, 2 - b]
+                    block = res_v[2 - a, 2 - b].astype(jnp.float32).T.astype(jnp.bfloat16)
                 else:
                     block = jnp.zeros((CH, CH), jnp.bfloat16)
-                wr_out[pl.ds(j * CH, CH), pl.ds((i * 3 + b) * CH, CH)] = block
-
-    for copy in act_copies:
-        copy.wait()
-    for d, (dh, ds) in enumerate(SIDES):
-        there = present(dh, ds)
-        if dh == 0:
-            sdrow[d] = silu_slope(rowland[d]) * there
-        elif ds == 0:
-            sdcol[d - 2, pl.ds(16, rows), :] = silu_slope(colland[d - 2]) * there
-        else:
-            tile = silu_slope(cornerland[d - 4]) * there
-            line = 15 if dh > 0 else 0
-            sdcol[0 if dh > 0 else 1, pl.ds(15 if ds > 0 else 16 + rows, 1), :] = tile[
-                line : line + 1
-            ]
+                wr_out[pl.ds((i * 3 + b) * CH, CH), pl.ds(j * CH, CH)] = block
 
     wanted = []
     for s in range(ns):
@@ -391,6 +352,28 @@
             device_id_type=MESH,
         ).start()
 
+    act_copies = []
+    for d, (dh, ds) in enumerate(SIDES):
+        if dh == 0:
+            src, dst = am_v.at[rows - 1 if ds > 0 else 0], rowland.at[d]
+        elif ds == 0:
+            src, dst = colmsg.at[1 if dh > 0 else 0], colland.at[d - 2]
+        else:
+            src = am_v.at[rows - 1 if ds > 0 else 0, pl.ds(CH - 16 if dh > 0 else 0, 16)]
+            dst = cornerland.at[d - 4]
+        act_copies.append(
+            pltpu.make_async_remote_copy(
+                src_ref=src,
+                dst_ref=dst,
+                send_sem=asend_sem.at[d],
+                recv_sem=arecv_sem.at[d],
+                device_id=(dp, lax.rem(hd + dh + nh, nh), lax.rem(sp + ds + ns, ns)),
+                device_id_type=MESH,
+            )
+        )
+    for copy in act_copies:
+        copy.start()
+
     low = lax.broadcasted_iota(jnp.int32, (8, 128), 1) < 64
 
     def lanes_of(spread, at, b):
@@ -403,6 +386,66 @@
     for b in range(PATCH):
         for r in range(ns):
             x_v[r + 1, pl.ds(16 + b, 8, stride=16), :] = lanes_of(spread, 8 * r, b)
+
+    x_v[0] = jnp.zeros((PADC, 128), jnp.float32)
+    lane = lax.broadcasted_iota(jnp.int32, (PADC, 128), 1)
+
+    def set_line(block, u):
+        line_f[u] = jnp.where(lane < 6, pltpu.roll(x_v[block], 80, 1), x_v[block + 1])
+
+    def left_side(u, start, size):
+        return jnp.concatenate(
+            [
+                line_f[u, pl.ds(start - 1, size), :]
+                + pltpu.roll(line_f[u, pl.ds(start, size), :], 64, 1),
+                line_f[u, pl.ds(start + 1, size), :],
+            ],
+            axis=1,
+        ).astype(jnp.bfloat16)
+
+    def inner(step, carry):
+        block = 2 * step
+        for u in range(2):
+            set_line(block + u, u)
+        lhs = jnp.concatenate([left_side(u, 16, CH) for u in range(2)], axis=0)
+        for t in range(8):
+            band = jnp.concatenate([band_v[2 * t], band_v[2 * t + 1]], axis=1)
+            act = jnp.dot(lhs, band, preferred_element_type=jnp.float32)
+            for u in range(2):
+                for i in range(2):
+                    slot = 2 * t + i
+                    r = jnp.maximum((block + u) * PATCH + slot - 1, 0)
+                    spot = u * PATCH + slot
+                    row_f[spot, pl.ds(8, CH), :] = act[
+                        CH * u : CH * u + CH, i * CH : (i + 1) * CH
+                    ] * am_v[r].astype(jnp.float32)
+                    for b in range(3):
+                        mid_out[(block + u) * 8 + t, i * 3 + b] = row_f[
+                            spot, pl.ds(7 + b, CH), :
+                        ].astype(jnp.bfloat16)
+        return carry
+
+    row_f[:, pl.ds(0, 8), :] = jnp.zeros((2 * PATCH, 8, 128), jnp.float32)
+    row_f[:, pl.ds(8 + CH, 8), :] = jnp.zeros((2 * PATCH, 8, 128), jnp.float32)
+    half = ns // 2
+    lax.fori_loop(0, half - half // 4, inner, 0)
+
+    seven = sq1.at[pl.ds(0, nh - 1)]
+    pltpu.make_async_copy(seven, seven, q_sem.at[1]).wait()
+    mine = dp * ns + sp
+    sq2[mine] = jnp.sum(sq1[...], axis=0)
+    for j in range(1, nd * ns):
+        other = lax.rem(mine + j, nd * ns)
+        pltpu.make_async_remote_copy(
+            src_ref=sq2.at[mine],
+            dst_ref=sq2.at[mine],
+            send_sem=q_sem.at[2],
+            recv_sem=q_sem.at[3],
+            device_id=(lax.div(other, ns), hd, lax.rem(other, ns)),
+            device_id_type=MESH,
+        ).start()
+
+    lax.fori_loop(half - half // 4, half, inner, 0)
 
     for copy in halo_copies:
         copy.wait()
@@ -423,68 +466,73 @@
                 continue
             for i in range(ns):
                 x_v[i + 1, pl.ds(column, 1), :] = tile[i : i + 1]
-
-    seven = sq1.at[pl.ds(0, nh - 1)]
-    pltpu.make_async_copy(seven, seven, q_sem.at[1]).wait()
-    mine = dp * ns + sp
-    sq2[mine] = jnp.sum(sq1[...], axis=0)
-    for j in range(1, nd * ns):
-        other = lax.rem(mine + j, nd * ns)
-        pltpu.make_async_remote_copy(
-            src_ref=sq2.at[mine],
-            dst_ref=sq2.at[mine],
-            send_sem=q_sem.at[2],
-            recv_sem=q_sem.at[3],
-            device_id=(lax.div(other, ns), hd, lax.rem(other, ns)),
-            device_id_type=MESH,
-        ).start()
-
-    lane = lax.broadcasted_iota(jnp.int32, (PADC, 128), 1)
-
-    def left_side(block, u):
-        line_f[u] = jnp.where(lane < 6, pltpu.roll(x_v[block], 80, 1), x_v[block + 1])
-        return jnp.concatenate(
-            [
-                line_f[u, pl.ds(7, 144), :] + pltpu.roll(line_f[u, pl.ds(8, 144), :], 64, 1),
-                line_f[u, pl.ds(9, 144), :],
-            ],
-            axis=1,
-        ).astype(jnp.bfloat16)
-
-    def pairs(block, blocks, count):
-        lhs = jnp.concatenate([left_side(block + u, u) for u in range(blocks)], axis=0)
-        for t in range(count):
-            band = jnp.concatenate([band_v[2 * t], band_v[2 * t + 1]], axis=1)
-            act = jnp.dot(lhs, band, preferred_element_type=jnp.float32)
-            for u in range(blocks):
-                for i in range(2):
-                    slot = 2 * t + i
-                    r = (block + u) * PATCH + slot - 1
-                    grad = act[144 * u : 144 * u + 144, i * CH : (i + 1) * CH]
-                    if slot == 0 and u == 0 and count > 1:
-                        slope = am_v[jnp.maximum(r, 0)].astype(jnp.float32)
-                        slope = jnp.where(r < 0, sdrow[0], slope)
-                    elif slot == 1 and count == 1:
-                        slope = sdrow[1]
+    for copy in act_copies:
+        copy.wait()
+    for d, (dh, ds) in enumerate(SIDES):
+        there = present(dh, ds)
+        if dh == 0:
+            sdrow[d] = rowland[d].astype(jnp.float32) * there
+        elif ds == 0:
+            sdcol[d - 2, pl.ds(16, rows), :] = colland[d - 2].astype(jnp.float32) * there
+        else:
+            tile = cornerland[d - 4].astype(jnp.float32) * there
+            line = 15 if dh > 0 else 0
+            sdcol[0 if dh > 0 else 1, pl.ds(15 if ds > 0 else 16 + rows, 1), :] = tile[
+                line : line + 1
+            ]
+
+    for block in range(ns):
+        set_line(block, block)
+        for side in range(2):
+            edge_v[pl.ds(64 * block + 32 * side, 32), :] = left_side(block, 8 + 112 * side, 32)
+
+    def edges(t, carry):
+        band = jnp.concatenate([band_v[2 * t], band_v[2 * t + 1]], axis=1)
+        act = jnp.dot(edge_v[...], band, preferred_element_type=jnp.float32)
+        for block in range(ns):
+            for i in range(2):
+                row = block * PATCH + 2 * t + i - 1
+                inside = jnp.maximum(row, 0)
+                for side in range(2):
+                    spot = (block * 2 + i) * 2 + side
+                    at = 64 * block + 32 * side
+                    grad = act[at : at + 32, i * CH : (i + 1) * CH]
+                    slope = am_v[inside, pl.ds((CH - 32) * side, 32), :].astype(jnp.float32)
+                    beyond = sdcol[side, pl.ds(row + 16, 1), :]
+                    if side == 0:
+                        fix_f[spot, pl.ds(0, 8), :] = grad[:8] * beyond
+                        fix_f[spot, pl.ds(8, 24), :] = grad[8:] * slope[:24]
                     else:
-                        slope = am_v[r].astype(jnp.float32)
-                    spot = u * PATCH + slot
-                    row_f[spot, pl.ds(0, 8), :] = grad[:8] * sdcol[0, pl.ds(r + 16, 1), :]
-                    row_f[spot, pl.ds(8, CH), :] = grad[8 : 8 + CH] * slope
-                    row_f[spot, pl.ds(8 + CH, 8), :] = (
-                        grad[8 + CH :] * sdcol[1, pl.ds(r + 16, 1), :]
-                    )
+                        fix_f[spot, pl.ds(0, 24), :] = grad[:24] * slope[8:]
+                        fix_f[spot, pl.ds(24, 8), :] = grad[24:] * beyond
                     for b in range(3):
-                        mid_out[(block + u) * 8 + t, :, pl.ds((i * 3 + b) * CH, CH)] = row_f[
-                            spot, pl.ds(7 + b, CH), :
+                        mid_out[block * 8 + t, i * 3 + b, pl.ds((CH - 16) * side, 16), :] = fix_f[
+                            spot, pl.ds(7 + b, 16), :
                         ].astype(jnp.bfloat16)
-
-    def first(block, carry):
-        pairs(2 * block, 2, 8)
         return carry
 
-    lax.fori_loop(0, ns // 2, first, 0)
-    pairs(ns, 1, 1)
+    lax.fori_loop(0, 8, edges, 0)
+
+    set_line(ns, ns)
+    band = jnp.concatenate([band_v[0], band_v[1]], axis=1)
+    lhs = jnp.concatenate([left_side(0, 8, 144), left_side(ns, 8, 144)], axis=0)
+    act = jnp.dot(lhs, band, preferred_element_type=jnp.float32)
+    for u in range(2):
+        for i in range(2):
+            row = u * rows + i - 1
+            grad = act[144 * u : 144 * u + 144, i * CH : (i + 1) * CH]
+            if u == i:
+                slope = sdrow[u]
+            else:
+                slope = am_v[row].astype(jnp.float32)
+            spot = 2 * u + i
+            row_f[spot, pl.ds(0, 8), :] = grad[:8] * sdcol[0, pl.ds(row + 16, 1), :]
+            row_f[spot, pl.ds(8, CH), :] = grad[8 : 8 + CH] * slope
+            row_f[spot, pl.ds(8 + CH, 8), :] = grad[8 + CH :] * sdcol[1, pl.ds(row + 16, 1), :]
+            for b in range(3):
+                mid_out[u * ns * 8, i * 3 + b] = row_f[spot, pl.ds(7 + b, CH), :].astype(
+                    jnp.bfloat16
+                )
 
     rest = sq2.at[pl.ds(0, nd * ns - 1)]
     pltpu.make_async_copy(rest, rest, q_sem.at[3]).wait()
@@ -498,27 +546,35 @@
 
 def decode_kernel(ns, entries, mid_ref, slope_ref, wr_ref, total, out, out_v, out_sem):
     scale = lax.rsqrt(jnp.sum(total[...], keepdims=True) / entries + 1e-06)
-
-    def second(g, carry):
-        near = mid_ref[pl.ds(8 * g, 8)].reshape(8 * CH, 6 * CH)
-        far = mid_ref[pl.ds(8 * g + 1, 8)].reshape(8 * CH, 6 * CH)
-        spread = lax.dot_general(
-            near, wr_ref[:, pl.ds(0, 6 * CH)], NT, preferred_element_type=jnp.float32
-        ) + lax.dot_general(
-            far, wr_ref[:, pl.ds(6 * CH, 6 * CH)], NT, preferred_element_type=jnp.float32
-        )
-        for q in range(8):
+    size = min(16, 8 * ns)
+
+    def step(g, carry):
+        terms = []
+        for late in range(2):
+            pieces = [
+                mid_ref[pl.ds(size * g + late, size), i].reshape(size * CH, CH) for i in range(6)
+            ]
+            terms.append(
+                jnp.dot(
+                    jnp.concatenate(pieces, axis=1),
+                    wr_ref[pl.ds(6 * CH * late, 6 * CH), :],
+                    preferred_element_type=jnp.float32,
+                )
+            )
+        spread = terms[0] + terms[1]
+        for q in range(size):
             for j in range(2):
-                row = g * PATCH + 2 * q + j
+                row = 2 * (g * size + q) + j
                 part = spread[q * CH : (q + 1) * CH, j * CH : (j + 1) * CH]
-                mid = mid_ref[8 * g + q + j, :, pl.ds((4 - 3 * j) * CH, CH)].astype(jnp.float32)
+                mid = mid_ref[size * g + q + j, 4 - 3 * j].astype(jnp.float32)
                 slope = slope_ref[row].astype(jnp.float32)
                 out_v[row] = (scale * (mid + slope * part)).astype(jnp.bfloat16)
-        part = pl.ds(g * PATCH, PATCH)
-        pltpu.make_async_copy(out_v.at[part], out.at[0, part], out_sem).start()
+            if q % 4 == 3:
+                done = pl.ds(2 * (g * size + q) - 6, 8)
+                pltpu.make_async_copy(out_v.at[done], out.at[0, done], out_sem).start()
         return carry
 
-    lax.fori_loop(0, ns, second, 0)
+    lax.fori_loop(0, 8 * ns // size, step, 0)
     pltpu.make_async_copy(out_v, out.at[0], out_sem).wait()
 
 
@@ -556,9 +612,9 @@
     mid, slope, wr, total = pl.pallas_call(
         functools.partial(trunk_kernel, nd, nh, ns, order, per),
         out_shape=(
-            pltpu.VMEM((8 * ns + 1, CH, 6 * CH), bf16),
+            pltpu.VMEM((8 * ns + 1, 6, CH, CH), bf16),
             pltpu.VMEM((rows, CH, CH), bf16),
-            pltpu.VMEM((2 * CH, 12 * CH), bf16),
+            pltpu.VMEM((12 * CH, 2 * CH), bf16),
             pltpu.VMEM((8, 128), f32),
         ),
         in_specs=[smem] + [pl.BlockSpec(memory_space=pltpu.HBM)] * 12,
@@ -580,7 +636,6 @@
             pltpu.VMEM((rows, CH, CH), bf16),
             pltpu.VMEM((patches, C), bf16),
             pltpu.VMEM((patches, C), f32),
-            pltpu.VMEM((2, rows, 16, CH), bf16),
             pltpu.VMEM((rows * 16, CH), f32),
             pltpu.VMEM((ns, nh, 16, HALF), bf16),
             pltpu.VMEM((group, 16, HALF), bf16),
@@ -595,11 +650,13 @@
             pltpu.VMEM((8 * ns, P3), f32),
             pltpu.VMEM((64, P3), f32),
             pltpu.VMEM((ns + 2, PADC, 128), f32),
-            pltpu.VMEM((2, PADC, 128), f32),
+            pltpu.VMEM((ns + 1, PADC, 128), f32),
             pltpu.VMEM((2 * PATCH, 144, 128), f32),
+            pltpu.VMEM((64 * ns, 256), bf16),
+            pltpu.VMEM((4 * ns, 32, 128), f32),
             pltpu.VMEM((nh, 8, 128), f32),
             pltpu.VMEM((nd * ns, 8, 128), f32),
-            dma((12,)),
+            dma((10,)),
             dma((2,)),
             dma,
             dma,

time: 44.7 us -> 41.3 us (0.924)
  Pallas kernels: 43.9 us -> 40.5 us
    pallas_call x1, Pallas kernels: 34.9 us -> 32.2 us  [local(): pl.pallas_call(functools.partial(trunk_kernel, nd, nh, ns, order, per), o...]
    pallas_call x1, Pallas kernels: 9.04 us -> 8.25 us  [local(): pl.pallas_call(functools.partial(decode_kernel, ns, float(nd * ns * ns *...]
where the time goes in v2:
time: 41.3 us; the launch traced here: 41.1 us
  Pallas kernels  40.5 us (98%)
  between operations  0.66 us (2%)
    pallas_call x1, Pallas kernels, local(): pl.pallas_call(functools.partial(trunk_kernel, nd, nh, ns, order, per), o...  32.2 us
    pallas_call x1, Pallas kernels, local(): pl.pallas_call(functools.partial(decode_kernel, ns, float(nd * ns * ns *...  8.25 us

profile of v2, /device:TPU:1, one launch (start us, length us, event | category | flops | bytes accessed | tf_op | source)
XLA Modules:
  0.0 41.1 jit_solution(12602216423465069693)
XLA Ops:
  0.7 32.2 %shard_map.127 = (bf16[65,6,128,128]{3,2,1,0:T(8,128)(2,1)S(1)}, bf16[128,128,128]{2,1,0:T(8,128)(2,1)S(1)}, bf16[1536,256]{1,0:T(8,128)(2,1)S(1)}, f32[8,128]{1,0:T(8,128)S(1)}) custom-call(s32[1,1]{1,0:T(1,128)S(6)} %copy.14.weight, s32[64]{0:T(128)} %map_hbm.1, bf16[1,8,64,1280]{3,2,1,0:T(8,128)(2,1)} %feats.1, f32[1280]{0:T(1024)} %gain_hbm.1, ...), custom_call_target="tpu_custom_call" | custom-call | tf_op jit(solution)/shard_map/pallas_call | solution.py:612
  32.9 8.3 %shard_map.128 = bf16[1,128,128,128]{3,2,1,0:T(8,128)(2,1)} custom-call(bf16[65,6,128,128]{3,2,1,0:T(8,128)(2,1)S(1)} %get-tuple-element.9.mid_ref, bf16[128,128,128]{2,1,0:T(8,128)(2,1)S(1)} %get-tuple-element.10.slope_ref, bf16[1536,256]{1,0:T(8,128)(2,1)S(1)} %get-tuple-element.11.wr_ref, f32[8,128]{1,0:T(8,128)S(1)} %get-tuple-element.12.total), custom_call_target="tpu_custom_call" | custom-call | tf_op jit(solution)/shard_map/pallas_call | solution.py:687

commit v3 on v2

--- a/solution.py
+++ b/solution.py
@@ -48,7 +48,7 @@
     nh,
     ns,
     order,
-    per,
+    chunks,
     weight,
     map_hbm,
     feats,
@@ -65,6 +65,7 @@
     mid_out,
     slope_out,
     wr_out,
+    part_out,
     total_out,
     row_map,
     f_v,
@@ -117,7 +118,6 @@
     group = nh * ns
     me = hd * ns + sp
     barrier = pltpu.get_barrier_semaphore()
-
     def load(src, dst, i):
         return pltpu.make_async_copy(src, dst, load_sem.at[i])
 
@@ -136,25 +136,12 @@
     for one in (load_map, load_f, load_g, load_b, load_w, load_hb, load_ho, load_e):
         one.start()
 
-    def greet(i, carry):
-        j = lax.rem(me + i, group)
-        pl.semaphore_signal(
-            barrier, inc=1, device_id=(dp, lax.div(j, ns), lax.rem(j, ns)), device_id_type=MESH
-        )
-        return carry
-
-    lax.fori_loop(1, group, greet, 0)
-
-    def greet_far(i, carry):
-        pl.semaphore_signal(
-            barrier,
-            inc=1,
-            device_id=(lax.rem(dp + 1 + lax.div(i, ns), nd), hd, lax.rem(i, ns)),
-            device_id_type=MESH,
-        )
-        return carry
-
-    lax.fori_loop(0, (nd - 1) * ns, greet_far, 0)
+    for i in range(1, group):
+        place = (dp, lax.rem(hd + i // ns, nh), lax.rem(sp + i % ns, ns))
+        pl.semaphore_signal(barrier, inc=1, device_id=place, device_id_type=MESH)
+    for i in range(ns, nd * ns):
+        place = (lax.rem(dp + i // ns, nd), hd, lax.rem(sp + i % ns, ns))
+        pl.semaphore_signal(barrier, inc=1, device_id=place, device_id_type=MESH)
 
     load_map.wait()
     load_g.wait()
@@ -202,15 +189,15 @@
                     device_id_type=MESH,
                 ).start()
 
-    for chunk in range(ns // per):
-        part = pl.ds(chunk * per * cols, per * cols)
+    for chunk, (start, per) in enumerate(chunks):
+        part = pl.ds(start * cols, per * cols)
         hidden = (
             jnp.dot(normed_v[part, :], w_v[...], preferred_element_type=jnp.float32) + first_bias
         )
         slopes = (second * gelu_slope(hidden)).astype(jnp.bfloat16)
         scaled = lax.dot_general(slopes, w_v[...], NT, preferred_element_type=jnp.float32) * gain
         unit = unit_v[part, :]
-        inverse = jnp.concatenate(inverses[chunk * per : chunk * per + per], axis=0)
+        inverse = jnp.concatenate(inverses[start : start + per], axis=0)
         patch = inverse * (
             scaled
             - jnp.mean(scaled, -1, keepdims=True)
@@ -228,11 +215,11 @@
         for t in range(per):
             for h in range(nh):
                 at = (t * nh + h) * STRIP
-                send[chunk * per + t, h] = stack(pixels[at : at + STRIP]).astype(jnp.bfloat16)
+                send[start + t, h] = stack(pixels[at : at + STRIP]).astype(jnp.bfloat16)
         if chunk == 0:
             pl.semaphore_wait(barrier, group - 1 + (nd - 1) * ns)
         for t in range(per):
-            send_rows(chunk * per + t)
+            send_rows(start + t)
 
     def present(dh, ds):
         inside = jnp.bool_(True)
@@ -427,8 +414,38 @@
 
     row_f[:, pl.ds(0, 8), :] = jnp.zeros((2 * PATCH, 8, 128), jnp.float32)
     row_f[:, pl.ds(8 + CH, 8), :] = jnp.zeros((2 * PATCH, 8, 128), jnp.float32)
-    half = ns // 2
-    lax.fori_loop(0, half - half // 4, inner, 0)
+    lax.fori_loop(0, ns // 2, inner, 0)
+
+    early, pairs = 2 * ns, 3 * ns
+
+    def convolve(begin, count, where):
+        terms = []
+        for late in range(2):
+            pieces = [
+                jnp.concatenate(
+                    [
+                        mid_out[pl.ds(begin + late, count), i, w, :].reshape(-1, CH)
+                        for w in where
+                    ],
+                    axis=0,
+                )
+                for i in range(6)
+            ]
+            terms.append(
+                jnp.dot(
+                    jnp.concatenate(pieces, axis=1),
+                    wr_out[pl.ds(6 * CH * late, 6 * CH), :],
+                    preferred_element_type=jnp.float32,
+                )
+            )
+        return terms[0] + terms[1]
+
+    def conv_early(g, carry):
+        spread = convolve(early + g * ns, ns, [pl.ds(0, CH)])
+        part_out[pl.ds(g * ns, ns)] = spread.reshape(ns, CH, 2 * CH)
+        return carry
+
+    lax.fori_loop(0, 1, conv_early, 0)
 
     seven = sq1.at[pl.ds(0, nh - 1)]
     pltpu.make_async_copy(seven, seven, q_sem.at[1]).wait()
@@ -445,10 +462,10 @@
             device_id_type=MESH,
         ).start()
 
-    lax.fori_loop(half - half // 4, half, inner, 0)
+    lax.fori_loop(1, pairs // ns, conv_early, 0)
 
     for copy in halo_copies:
-        copy.wait()
+        copy.wait_recv()
     for d, (dh, ds) in enumerate(SIDES):
         hp[pl.ds(8 * d, 8), :] = unstack(hland[d].astype(jnp.float32) * present(dh, ds))
     spread = jnp.dot(hp[...].astype(jnp.bfloat16), t_v[...], preferred_element_type=jnp.float32)
@@ -467,7 +484,7 @@
             for i in range(ns):
                 x_v[i + 1, pl.ds(column, 1), :] = tile[i : i + 1]
     for copy in act_copies:
-        copy.wait()
+        copy.wait_recv()
     for d, (dh, ds) in enumerate(SIDES):
         there = present(dh, ds)
         if dh == 0:
@@ -511,7 +528,8 @@
                         ].astype(jnp.bfloat16)
         return carry
 
-    lax.fori_loop(0, 8, edges, 0)
+    for t in range(8):
+        edges(t, 0)
 
     set_line(ns, ns)
     band = jnp.concatenate([band_v[0], band_v[1]], axis=1)
@@ -534,9 +552,17 @@
                     jnp.bfloat16
                 )
 
+    strips = convolve(early, pairs, [pl.ds(0, 16), pl.ds(CH - 16, 16)])
+    for side in range(2):
+        part_out[:, pl.ds((CH - 16) * side, 16), :] = strips[
+            side * pairs * 16 : (side + 1) * pairs * 16
+        ].reshape(pairs, 16, 2 * CH)
+
     rest = sq2.at[pl.ds(0, nd * ns - 1)]
     pltpu.make_async_copy(rest, rest, q_sem.at[3]).wait()
     total_out[...] = jnp.sum(sq2[...], axis=0)
+    for copy in halo_copies + act_copies:
+        copy.wait_send()
     pltpu.make_async_copy(rest, rest, q_sem.at[2]).wait()
     pltpu.make_async_copy(seven, seven, q_sem.at[0]).wait()
     pltpu.make_async_copy(
@@ -544,15 +570,26 @@
     ).wait()
 
 
-def decode_kernel(ns, entries, mid_ref, slope_ref, wr_ref, total, out, out_v, out_sem):
+def decode_kernel(ns, entries, mid_ref, slope_ref, wr_ref, part_ref, total, out, out_v, out_sem):
     scale = lax.rsqrt(jnp.sum(total[...], keepdims=True) / entries + 1e-06)
-    size = min(16, 8 * ns)
-
-    def step(g, carry):
+    early, pairs = 2 * ns, 3 * ns
+
+    def finish(p, pair):
+        for j in range(2):
+            mid = mid_ref[p + j, 4 - 3 * j].astype(jnp.float32)
+            slope = slope_ref[2 * p + j].astype(jnp.float32)
+            part = pair[:, j * CH : (j + 1) * CH]
+            out_v[2 * p + j] = (scale * (mid + slope * part)).astype(jnp.bfloat16)
+        if p % 4 == 3:
+            done = pl.ds(2 * p - 6, 8)
+            pltpu.make_async_copy(out_v.at[done], out.at[0, done], out_sem).start()
+
+    ready = list(range(early, early + pairs))
+    for begin, size in ((0, 2 * ns), (early + pairs, 2 * ns), (early + pairs + 2 * ns, ns)):
         terms = []
         for late in range(2):
             pieces = [
-                mid_ref[pl.ds(size * g + late, size), i].reshape(size * CH, CH) for i in range(6)
+                mid_ref[pl.ds(begin + late, size), i].reshape(size * CH, CH) for i in range(6)
             ]
             terms.append(
                 jnp.dot(
@@ -561,20 +598,12 @@
                     preferred_element_type=jnp.float32,
                 )
             )
+        for p in ready[: pairs // 3]:
+            finish(p, part_ref[p - early])
+        ready = ready[pairs // 3 :]
         spread = terms[0] + terms[1]
         for q in range(size):
-            for j in range(2):
-                row = 2 * (g * size + q) + j
-                part = spread[q * CH : (q + 1) * CH, j * CH : (j + 1) * CH]
-                mid = mid_ref[size * g + q + j, 4 - 3 * j].astype(jnp.float32)
-                slope = slope_ref[row].astype(jnp.float32)
-                out_v[row] = (scale * (mid + slope * part)).astype(jnp.bfloat16)
-            if q % 4 == 3:
-                done = pl.ds(2 * (g * size + q) - 6, 8)
-                pltpu.make_async_copy(out_v.at[done], out.at[0, done], out_sem).start()
-        return carry
-
-    lax.fori_loop(0, 8 * ns // size, step, 0)
+            finish(begin + q, spread[q * CH : (q + 1) * CH])
     pltpu.make_async_copy(out_v, out.at[0], out_sem).wait()
 
 
@@ -603,22 +632,23 @@
     patches = ns * nh * STRIP
     order = [s % ns for s in (2, -2, 3, -3, 4, 1, -1)]
     order = [s for i, s in enumerate(order) if s and s not in order[:i]] + [0]
-    per = max(1, ns // 2)
+    chunks = [(0, ns // 2), (ns // 2, ns - ns // 2)]
     f32, bf16 = jnp.float32, jnp.bfloat16
     vmem = pl.BlockSpec(memory_space=pltpu.VMEM)
     smem = pl.BlockSpec(memory_space=pltpu.SMEM)
     hbm = pl.BlockSpec(memory_space=pl.ANY)
     dma = pltpu.SemaphoreType.DMA
-    mid, slope, wr, total = pl.pallas_call(
-        functools.partial(trunk_kernel, nd, nh, ns, order, per),
+    mid, slope, wr, part, total = pl.pallas_call(
+        functools.partial(trunk_kernel, nd, nh, ns, order, chunks),
         out_shape=(
             pltpu.VMEM((8 * ns + 1, 6, CH, CH), bf16),
             pltpu.VMEM((rows, CH, CH), bf16),
             pltpu.VMEM((12 * CH, 2 * CH), bf16),
+            pltpu.VMEM((3 * ns, CH, 2 * CH), f32),
             pltpu.VMEM((8, 128), f32),
         ),
         in_specs=[smem] + [pl.BlockSpec(memory_space=pltpu.HBM)] * 12,
-        out_specs=(vmem,) * 4,
+        out_specs=(vmem,) * 5,
         scratch_shapes=[
             pltpu.SMEM(row_map.shape, jnp.int32),
             pltpu.VMEM(features.shape[1:], bf16),
@@ -687,11 +717,11 @@
     return pl.pallas_call(
         functools.partial(decode_kernel, ns, float(nd * ns * ns * nh * STRIP * P3)),
         out_shape=jax.ShapeDtypeStruct(act_in.shape, bf16),
-        in_specs=[vmem] * 4,
+        in_specs=[vmem] * 5,
         out_specs=hbm,
         scratch_shapes=[pltpu.VMEM((rows, CH, CH), bf16), dma],
         compiler_params=pltpu.CompilerParams(vmem_limit_bytes=16 * 1024 * 1024),
-    )(mid, slope, wr, total)
+    )(mid, slope, wr, part, total)
 
 
 def solution(mesh):

time: 41.3 us -> 39.5 us (0.956)
  Pallas kernels: 40.5 us -> 38.5 us
    pallas_call x1, Pallas kernels: 8.25 us -> 5.75 us  [local(): pl.pallas_call(functools.partial(decode_kernel, ns, float(nd * ns * ns *...]
    pallas_call x1, Pallas kernels: 32.2 us -> 32.8 us  [local(): pl.pallas_call(functools.partial(trunk_kernel, nd, nh, ns, order, chunks)...]
where the time goes in v3:
time: 39.5 us; the launch traced here: 39.4 us
  Pallas kernels  38.5 us (97%)
  between operations  0.82 us (2%)
    pallas_call x1, Pallas kernels, local(): pl.pallas_call(functools.partial(trunk_kernel, nd, nh, ns, order, chunks)...  32.8 us
    pallas_call x1, Pallas kernels, local(): pl.pallas_call(functools.partial(decode_kernel, ns, float(nd * ns * ns *...  5.75 us

profile of v3, /device:TPU:1, one launch (start us, length us, event | category | flops | bytes accessed | tf_op | source)
XLA Modules:
  0.0 39.4 jit_solution(10970521756195726206)
XLA Ops:
  0.7 32.8 %shard_map.127 = (bf16[65,6,128,128]{3,2,1,0:T(8,128)(2,1)S(1)}, bf16[128,128,128]{2,1,0:T(8,128)(2,1)S(1)}, bf16[1536,256]{1,0:T(8,128)(2,1)S(1)}, f32[24,128,256]{2,1,0:T(8,128)S(1)}, f32[8,128]{1,0:T(8,128)S(1)}) custom-call(s32[1,1]{1,0:T(1,128)S(6)} %copy.14.weight, s32[64]{0:T(128)} %map_hbm.1, bf16[1,8,64,1280]{3,2,1,0:T(8,128)(2,1)} %feats.1, ...), custom_call_target="tpu_custom_call" | custom-call | tf_op jit(solution)/shard_map/pallas_call | solution.py:641
  33.5 5.7 %shard_map.128 = bf16[1,128,128,128]{3,2,1,0:T(8,128)(2,1)} custom-call(bf16[65,6,128,128]{3,2,1,0:T(8,128)(2,1)S(1)} %get-tuple-element.10.mid_ref, bf16[128,128,128]{2,1,0:T(8,128)(2,1)S(1)} %get-tuple-element.11.slope_ref, bf16[1536,256]{1,0:T(8,128)(2,1)S(1)} %get-tuple-element.12.wr_ref, f32[24,128,256]{2,1,0:T(8,128)S(1)} %get-tuple-element.13.part_ref, ...), custom_call_target="tpu_custom_call" | custom-call | tf_op jit(solution)/shard_map/pallas_call | solution.py:717

commit v4 on v3

--- a/solution.py
+++ b/solution.py
@@ -390,15 +390,17 @@
             axis=1,
         ).astype(jnp.bfloat16)
 
+    wide = min(4, ns)
+
     def inner(step, carry):
-        block = 2 * step
-        for u in range(2):
+        block = wide * step
+        for u in range(wide):
             set_line(block + u, u)
-        lhs = jnp.concatenate([left_side(u, 16, CH) for u in range(2)], axis=0)
+        lhs = jnp.concatenate([left_side(u, 16, CH) for u in range(wide)], axis=0)
         for t in range(8):
             band = jnp.concatenate([band_v[2 * t], band_v[2 * t + 1]], axis=1)
             act = jnp.dot(lhs, band, preferred_element_type=jnp.float32)
-            for u in range(2):
+            for u in range(wide):
                 for i in range(2):
                     slot = 2 * t + i
                     r = jnp.maximum((block + u) * PATCH + slot - 1, 0)
@@ -412,9 +414,9 @@
                         ].astype(jnp.bfloat16)
         return carry
 
-    row_f[:, pl.ds(0, 8), :] = jnp.zeros((2 * PATCH, 8, 128), jnp.float32)
-    row_f[:, pl.ds(8 + CH, 8), :] = jnp.zeros((2 * PATCH, 8, 128), jnp.float32)
-    lax.fori_loop(0, ns // 2, inner, 0)
+    row_f[:, pl.ds(0, 8), :] = jnp.zeros((wide * PATCH, 8, 128), jnp.float32)
+    row_f[:, pl.ds(8 + CH, 8), :] = jnp.zeros((wide * PATCH, 8, 128), jnp.float32)
+    lax.fori_loop(0, ns // wide, inner, 0)
 
     early, pairs = 2 * ns, 3 * ns
 
@@ -681,7 +683,7 @@
             pltpu.VMEM((64, P3), f32),
             pltpu.VMEM((ns + 2, PADC, 128), f32),
             pltpu.VMEM((ns + 1, PADC, 128), f32),
-            pltpu.VMEM((2 * PATCH, 144, 128), f32),
+            pltpu.VMEM((min(4, ns) * PATCH, 144, 128), f32),
             pltpu.VMEM((64 * ns, 256), bf16),
             pltpu.VMEM((4 * ns, 32, 128), f32),
             pltpu.VMEM((nh, 8, 128), f32),

time: 39.5 us -> 39 us (0.987)
  Pallas kernels: 38.5 us -> 38.1 us
    pallas_call x1, Pallas kernels: 32.8 us -> 32.3 us  [local(): pl.pallas_call(functools.partial(trunk_kernel, nd, nh, ns, order, chunks)...]
where the time goes in v4:
time: 39 us; the launch traced here: 38.9 us
  Pallas kernels  38.1 us (98%)
  between operations  0.82 us (2%)
    pallas_call x1, Pallas kernels, local(): pl.pallas_call(functools.partial(trunk_kernel, nd, nh, ns, order, chunks)...  32.3 us
    pallas_call x1, Pallas kernels, local(): pl.pallas_call(functools.partial(decode_kernel, ns, float(nd * ns * ns *...  5.75 us

profile of v4, /device:TPU:1, one launch (start us, length us, event | category | flops | bytes accessed | tf_op | source)
XLA Modules:
  0.0 38.9 jit_solution(2310731180081215710)
XLA Ops:
  0.7 32.3 %shard_map.127 = (bf16[65,6,128,128]{3,2,1,0:T(8,128)(2,1)S(1)}, bf16[128,128,128]{2,1,0:T(8,128)(2,1)S(1)}, bf16[1536,256]{1,0:T(8,128)(2,1)S(1)}, f32[24,128,256]{2,1,0:T(8,128)S(1)}, f32[8,128]{1,0:T(8,128)S(1)}) custom-call(s32[1,1]{1,0:T(1,128)S(6)} %copy.14.weight, s32[64]{0:T(128)} %map_hbm.1, bf16[1,8,64,1280]{3,2,1,0:T(8,128)(2,1)} %feats.1, ...), custom_call_target="tpu_custom_call" | custom-call | tf_op jit(solution)/shard_map/pallas_call | solution.py:643
  33.0 5.8 %shard_map.128 = bf16[1,128,128,128]{3,2,1,0:T(8,128)(2,1)} custom-call(bf16[65,6,128,128]{3,2,1,0:T(8,128)(2,1)S(1)} %get-tuple-element.10.mid_ref, bf16[128,128,128]{2,1,0:T(8,128)(2,1)S(1)} %get-tuple-element.11.slope_ref, bf16[1536,256]{1,0:T(8,128)(2,1)S(1)} %get-tuple-element.12.wr_ref, f32[24,128,256]{2,1,0:T(8,128)S(1)} %get-tuple-element.13.part_ref, ...), custom_call_target="tpu_custom_call" | custom-call | tf_op jit(solution)/shard_map/pallas_call | solution.py:719
